TPU v7x, 256 devices: a whole 4x4x8 slice. The times are simulated.
256 devices in a mesh: gx: 8 (over z), gy: 32 (over y, x, core).
Axes of the slice: x: 4, y: 4, z: 8, core: 2. Of those that a mesh axis runs over, the one named last changes fastest.
Arguments:
- tokens: bfloat16 [512, 8192], P('gy', 'gx'), may hold values from -6 to 6
- gate_weight: bfloat16 [8192, 28672], P('gx', 'gy'), may hold values from -0.0625 to 0.0625
- up_weight: bfloat16 [8192, 28672], P('gx', 'gy'), may hold values from -0.0625 to 0.0625
- down_weight: bfloat16 [28672, 8192], P('gy', 'gx'), may hold values from -0.03125 to 0.03125
- out_grad: bfloat16 [512, 8192], P('gy', 'gx'), may hold values from -6 to 6
Outputs:
- input_grad: bfloat16 [512, 8192], P('gy', 'gx')
- gate_grad: bfloat16 [8192, 28672], P('gx', 'gy')
- up_grad: bfloat16 [8192, 28672], P('gx', 'gy')
- down_grad: bfloat16 [28672, 8192], P('gy', 'gx')
- grad_peaks: float32 [2], replicated
All inputs are finite; a program needn't handle non-finite values.
Results may differ from a plain program's by a relative error of at most 0.03.
Values may be sent and summed in bfloat16 or wider, within the bound.
A program may use at most 64 MiB of HBM per device.

v0:
```python
import jax
import jax.numpy as jnp
from jax import lax
from jax.sharding import PartitionSpec as P

FP8_MAX = 57344.0
HEADROOM = 8.0


def silu_parts(gate):
    sigma = jax.nn.sigmoid(gate)
    return (gate * sigma, sigma * (1.0 + gate * (1.0 - sigma)))


def hidden_grads(hidden_grad, gate, up_val):
    act, slope = silu_parts(gate)
    return (hidden_grad * up_val * slope, hidden_grad * act)


def saturate(values, safe_peak):
    scaled = values * (HEADROOM * FP8_MAX / safe_peak)
    return jnp.clip(scaled, -FP8_MAX, FP8_MAX).astype(jnp.bfloat16)


def local(tokens, gate_weight, up_weight, down_weight, out_grad):
    tok_all, grad_all = (
        lax.all_gather(tokens, "gy", axis=0, tiled=True),
        lax.all_gather(out_grad, "gy", axis=0, tiled=True),
    )
    gate_part = jnp.dot(tok_all, gate_weight, preferred_element_type=jnp.float32)
    up_part = jnp.dot(tok_all, up_weight, preferred_element_type=jnp.float32)
    contract = (((1,), (1,)), ((), ()))
    down_part = lax.dot_general(grad_all, down_weight, contract, preferred_element_type=jnp.float32)
    gate, up_val = (
        lax.psum(gate_part.astype(jnp.bfloat16), "gx").astype(jnp.float32),
        lax.psum(up_part.astype(jnp.bfloat16), "gx").astype(jnp.float32),
    )
    act, slope = silu_parts(gate)
    hidden = (act * up_val).astype(jnp.bfloat16)
    hidden_grad = lax.psum(down_part.astype(jnp.bfloat16), "gx").astype(jnp.float32)
    pre_gate, pre_up = hidden_grads(hidden_grad, gate, up_val)
    peak_gate, peak_up = lax.pmax((jnp.max(jnp.abs(pre_gate)), jnp.max(jnp.abs(pre_up))), "gy")
    coded_gate = saturate(pre_gate, peak_gate + 1e-06)
    coded_up = saturate(pre_up, peak_up + 1e-06)
    back_gate = (peak_gate + 1e-06) / (HEADROOM * FP8_MAX)
    back_up = (peak_up + 1e-06) / (HEADROOM * FP8_MAX)
    first = lax.dot_general(coded_gate, gate_weight, contract, preferred_element_type=jnp.float32)
    second = lax.dot_general(coded_up, up_weight, contract, preferred_element_type=jnp.float32)
    input_grad = lax.psum_scatter(
        (back_gate * first + back_up * second).astype(jnp.bfloat16),
        "gy",
        scatter_dimension=0,
        tiled=True,
    )
    rows = (((0,), (0,)), ((), ()))
    gate_grad = (
        back_gate * lax.dot_general(tok_all, coded_gate, rows, preferred_element_type=jnp.float32)
    ).astype(jnp.bfloat16)
    up_grad = (
        back_up * lax.dot_general(tok_all, coded_up, rows, preferred_element_type=jnp.float32)
    ).astype(jnp.bfloat16)
    down_grad = lax.dot_general(hidden, grad_all, rows, preferred_element_type=jnp.float32).astype(
        jnp.bfloat16
    )
    return (input_grad, gate_grad, up_grad, down_grad, jnp.stack([peak_gate, peak_up]))


def solution(mesh):
    in_specs = (P("gy", "gx"), P("gx", "gy"), P("gx", "gy"), P("gy", "gx"), P("gy", "gx"))
    out_specs = (P("gy", "gx"), P("gx", "gy"), P("gx", "gy"), P("gy", "gx"), P())
    return jax.shard_map(local, mesh=mesh, in_specs=in_specs, out_specs=out_specs, check_vma=False)
```

profile of v0, /device:TPU:1, one launch (start us, length us, event | category | flops | bytes accessed | tf_op | source)
XLA Modules:
  0.0 364.5 jit_solution(14702746672488839662)
XLA Ops:
  7.2 0.0 all-gather.5.cloned.1.call-start
  7.2 0.7 all-gather.5.cloned.1.call-update
  7.9 0.0 all-gather.3.cloned.1.call-start
  8.0 0.7 all-gather.3.cloned.1.call-update
  8.7 0.0 all-reduce.4.cloned.1.call-start
  8.7 53.9 %all-gather.5.cloned.1.call-done = bf16[512,1024]{1,0:T(8,128)(2,1)} async-done(((bf16[16,1024]{1,0:T(8,128)(2,1)}), bf16[512,1024]{1,0:T(8,128)(2,1)}) %all-gather.5.cloned.1.call-update) | async-done | bytes 1048592 | tf_op jit(solution)/shard_map/all_gather | solution.py:27
  62.6 4.1 %convolution_convert_fusion.2 = bf16[512,896]{1,0:T(8,128)(2,1)} fusion(bf16[512,1024]{1,0:T(8,128)(2,1)} %all-gather.5.cloned.1.call-done, bf16[1024,896]{1,0:T(8,128)(2,1)} %param.7), kind=kOutput, calls=%fused_computation.24 | convolution fusion | flops 939982848 | bytes 3801088 | tf_op jit(solution)/shard_map/dot_general | solution.py:31
  66.7 2.2 convolution_convert_fusion.1
  68.9 43.5 %all-gather.3.cloned.1.call-done = bf16[512,1024]{1,0:T(8,128)(2,1)} async-done(((bf16[16,1024]{1,0:T(8,128)(2,1)}), bf16[512,1024]{1,0:T(8,128)(2,1)}) %all-gather.3.cloned.1.call-update) | async-done | bytes 1048592 | tf_op jit(solution)/shard_map/all_gather | solution.py:28
  112.4 4.0 %convolution_convert_fusion.3 = bf16[512,896]{1,0:T(8,128)(2,1)} fusion(bf16[512,1024]{1,0:T(8,128)(2,1)} %all-gather.3.cloned.1.call-done, bf16[896,1024]{1,0:T(8,128)(2,1)} %param.8), kind=kOutput, calls=%fused_computation.25 | convolution fusion | flops 939982848 | bytes 3801088 | tf_op jit(solution)/shard_map/dot_general | solution.py:33
  116.4 0.0 all-reduce.4.cloned.1.call-update
  116.4 0.0 reduce-scatter.2.cloned.1.call-start
  116.5 84.6 %all-reduce.4.cloned.1.call-done = (bf16[512,896]{1,0:T(8,128)(2,1)}, bf16[512,896]{1,0:T(8,128)(2,1)}, bf16[512,896]{1,0:T(8,128)(2,1)}) async-done(((bf16[512,896]{1,0:T(8,128)(2,1)}, bf16[512,896]{1,0:T(8,128)(2,1)}, bf16[512,896]{1,0:T(8,128)(2,1)}), (bf16[512,896]{1,0:T(8,128)(2,1)}, bf16[512,896]{1,0:T(8,128)(2,1)}, bf16[512,896]{1,0:T(8,128)(2,1)})) %all-reduce.4.cloned.1.call-update) | async-done | bytes 2752528 | tf_op jit(solution)/shard_map/psum | solution.py:36
  201.1 4.5 %abs_reduce_fusion.1 = (f32[]{:T(128)}, f32[512,896]{1,0:T(8,128)}, f32[]{:T(128)}) fusion(bf16[512,896]{1,0:T(8,128)(2,1)} %get-tuple-element.14, bf16[512,896]{1,0:T(8,128)(2,1)} %get-tuple-element.12, bf16[512,896]{1,0:T(8,128)(2,1)} %get-tuple-element.13), kind=kLoop, calls=%fused_computation.19 | loop fusion | flops 8257534 | bytes 4587528 | tf_op jit(solution)/shard_map/reduce_max | solution.py:42
  205.6 65.5 %all-reduce = (f32[]{:T(128)}, f32[]{:T(128)}) all-reduce(f32[]{:T(128)} %get-tuple-element.15, f32[]{:T(128)} %get-tuple-element.17), channel_id=1, replica_groups=mesh['gx'=8,'gy'=32] {'gy'}, use_global_device_ids=true, to_apply=%region_4.0 | all-reduce | flops 2 | bytes 16 | tf_op jit(solution)/shard_map/pmax | solution.py:42
  272.5 2.9 fusion.10
  275.4 2.5 add_convert_fusion
  278.0 4.2 %fusion.7 = bf16[1024,896]{0,1:T(8,128)(2,1)} fusion(bf16[512,1024]{1,0:T(8,128)(2,1)} %all-gather.5.cloned.1.call-done, f32[]{:T(128)S(6)} %div.17, f32[512,896]{1,0:T(8,128)} %get-tuple-element.16, f32[]{:T(128)S(6)} %div.18), kind=kOutput, calls=%fused_computation.21 | convolution fusion | flops 942735360 | bytes 4718600 | tf_op jit(solution)/shard_map/dot_general | solution.py:57
  282.1 3.8 %copy.10 = bf16[1024,896]{1,0:T(8,128)(2,1)} copy(bf16[1024,896]{0,1:T(8,128)(2,1)} %fusion.7) | data formatting | bytes 3670016
  285.9 4.2 %fusion.8 = bf16[1024,896]{0,1:T(8,128)(2,1)} fusion(bf16[512,1024]{1,0:T(8,128)(2,1)} %all-gather.5.cloned.1.call-done, f32[]{:T(128)S(6)} %div.19, bf16[512,896]{1,0:T(8,128)(2,1)} %get-tuple-element.13, f32[]{:T(128)S(6)} %div.20, bf16[512,896]{1,0:T(8,128)(2,1)S(1)} %copy-done.2), kind=kOutput, calls=%fused_computation.22 | convolution fusion | flops 945946624 | bytes 4718600 | tf_op jit(solution)/shard_map/dot_general | solution.py:60
  290.1 3.9 %copy.11 = bf16[1024,896]{1,0:T(8,128)(2,1)} copy(bf16[1024,896]{0,1:T(8,128)(2,1)} %fusion.8) | data formatting | bytes 3670016
  294.0 1.8 pad_maximum_fusion
  295.9 4.0 %convolution_convert_fusion = bf16[896,1024]{1,0:T(8,128)(2,1)} fusion(bf16[512,1024]{1,0:T(8,128)(2,1)} %all-gather.3.cloned.1.call-done, bf16[512,896]{1,0:T(8,128)(2,1)S(1)} %copy-done.1, bf16[512,896]{1,0:T(8,128)(2,1)} %get-tuple-element.14), kind=kOutput, calls=%fused_computation.20 | convolution fusion | flops 944111616 | bytes 4718592 | tf_op jit(solution)/shard_map/dot_general | solution.py:62
  299.9 58.1 %reduce-scatter.2.cloned.1.call-done = bf16[16,1024]{1,0:T(8,128)(2,1)} async-done(((bf16[512,1024]{1,0:T(8,128)(2,1)}), bf16[16,1024]{1,0:T(8,128)(2,1)}) %reduce-scatter.2.cloned.1.call-update) | async-done | bytes 32784 | tf_op jit(solution)/shard_map/reduce_scatter | solution.py:49
  (13 shorter events, 0.0 us)
Async XLA Ops:
  7.2 59.5 %copy-start = (bf16[1024,896]{1,0:T(8,128)(2,1)S(1)}, bf16[1024,896]{1,0:T(8,128)(2,1)}, u32[]{:S(2)}) copy-start(bf16[1024,896]{1,0:T(8,128)(2,1)} %param.6) | copy-start | bytes 5505028
  7.2 55.4 %all-gather.5.cloned.1.call-start = ((), (), s32[]{:S(2)}) async-start(), calls=%async_computation.2 | async-start | bytes 1081344 | tf_op jit(solution)/shard_map/all_gather | solution.py:27
  7.9 104.5 %all-gather.3.cloned.1.call-start = ((), (), s32[]{:S(2)}) async-start(), calls=%async_computation.1 | async-start | bytes 1081344 | tf_op jit(solution)/shard_map/all_gather | solution.py:28
  8.7 192.4 %all-reduce.4.cloned.1.call-start = ((), (), s32[]{:S(2)}) async-start(), calls=%async_computation.4 | async-start | bytes 5505024 | tf_op jit(solution)/shard_map/psum | solution.py:36
  62.6 4.1 %copy-start.5 = (bf16[512,1024]{1,0:T(8,128)(2,1)S(1)}, bf16[512,1024]{1,0:T(8,128)(2,1)}, u32[]{:S(2)}) copy-start(bf16[512,1024]{1,0:T(8,128)(2,1)} %all-gather.5.cloned.1.call-done) | copy-start | bytes 3145732
  116.4 241.5 %reduce-scatter.2.cloned.1.call-start = ((), (), s32[]{:S(2)}) async-start(), calls=%async_computation.3 | async-start | bytes 1081344 | tf_op jit(solution)/shard_map/reduce_scatter | solution.py:49
  272.4 3.0 copy-start.2
  272.5 3.0 copy-start.3
  272.5 3.0 copy-start.4
  290.1 5.7 %copy-start.1 = (bf16[512,896]{1,0:T(8,128)(2,1)S(1)}, bf16[512,896]{1,0:T(8,128)(2,1)}, u32[]{:S(2)}) copy-start(bf16[512,896]{1,0:T(8,128)(2,1)} %get-tuple-element.12) | copy-start | bytes 2752516
Sparse Core Ops, SparseCore 0:
  10.6 52.0 all-gather.4
  65.2 47.1 all-gather.2
  116.6 84.5 all-reduce.3
  278.1 79.8 reduce-scatter.1
where the time goes:
time: 365 us
  waiting for transfers between devices  242 us (66%)
  blocking collectives  65.5 us (18%)
  matrix products  28.1 us (8%)
  between operations  15.2 us (4%)
  local copies, waits for them, and re-layouts  7.72 us (2%)
  other arithmetic  6.35 us (2%)
    psum x1, waiting for transfers between devices, local(): lax.psum(up_part.astype(jnp.bfloat16), 'gx').astype(jnp.float32)  84.6 us
    pmax x1, blocking collectives, local(): lax.pmax((jnp.max(jnp.abs(pre_gate)), jnp.max(jnp.abs(pre_up))), 'gy')  65.5 us
    reduce_scatter x1, waiting for transfers between devices, local(): lax.psum_scatter((back_gate * first + back_up * second).astype(jnp.bfloat...  58.1 us
    all_gather x1, waiting for transfers between devices, local(): lax.all_gather(tokens, 'gy', axis=0, tiled=True)  53.9 us
    all_gather x1, waiting for transfers between devices, local(): lax.all_gather(out_grad, 'gy', axis=0, tiled=True)  43.5 us
    unnamed x14, local copies, waits for them, and re-layouts  7.72 us
  transfers between devices with their start and end apart: 4, of which 4 were waited for; matrix products, arithmetic and copies ran while one was open for 8% of the time, Pallas kernels for 0%

commit v1 on v0

v1 whole, which is shorter than its diff:
```python
import functools

import jax
import jax.numpy as jnp
from jax import lax
from jax.experimental import pallas as pl
from jax.experimental.pallas import tpu as pltpu
from jax.sharding import PartitionSpec as P

MESH = pl.DeviceIdType.MESH
FP8_MAX = 57344.0
HEADROOM = 8.0
TOP = HEADROOM * FP8_MAX
NZ, NY, NX, ROWS = 8, 4, 4, 16
GROUPS = (0, 1, 3, 2)
GATE, UP, HGRAD = 0, 1, 2
PRE_GATE, HIDDEN, PRE_UP = 0, 1, 2


def dot(a, b):
    return jnp.dot(a, b, preferred_element_type=jnp.float32)


def device(z, y, x, c):
    return (lax.rem(z + NZ, NZ), (lax.rem(y + NY, NY) * NX + lax.rem(x + NX, NX)) * 2 + c)


def main_kernel(
    tok_hbm, grad_hbm, wg_hbm, wu_hbm, wd_hbm,
    ig_ref, peak_ref, tok_out, grad_out, back_out,
    xy, wg, wu, wd, wdt, wgt, wut, part, rs_send, rs_recv, back, coded, ig_part, ig_recv, row_sum, row_recv,
    pk, pk_recv,
    w_sem, x_send, x_recv, f_send, f_recv, y_send, y_recv, g_send, g_recv,
    r_send, r_recv, a_send, a_recv, p_send, p_recv, c_send, c_recv, d_send, d_recv, o_sem,
):
    z, gy = lax.axis_index("gx"), lax.axis_index("gy")
    y, x, c = gy // 8, lax.rem(gy // 2, NX), lax.rem(gy, 2)
    mine = c * NX + x
    partner = device(z, y, x, 1 - c)
    ups = (device(z + 1, y, x, c), device(z - 1, y, x, c))
    sends = []

    def remote(src, dst, s_sem, r_sem, dev):
        return pltpu.make_async_remote_copy(
            src_ref=src, dst_ref=dst, send_sem=s_sem, recv_sem=r_sem, device_id=dev, device_id_type=MESH
        )

    def send(src, dst, s_sem, r_sem, dev):
        copy = remote(src, dst, s_sem, r_sem, dev)
        copy.start()
        sends.append(copy)

    def arrived(ref, s_sem, r_sem):
        remote(ref, ref, s_sem, r_sem, partner).wait_recv()

    def rows(j, n=1):
        return pl.ds(pl.multiple_of(j * ROWS, ROWS), n * ROWS)

    def chunk(k):
        return lax.rem(z + k + 2 * NZ, NZ)

    w_copies = [
        pltpu.make_async_copy(src, dst, w_sem.at[i])
        for i, (src, dst) in enumerate(
            ((tok_hbm, xy.at[0, 0, rows(mine)]), (grad_hbm, xy.at[1, 0, rows(mine)]), (wd_hbm, wd), (wg_hbm, wg), (wu_hbm, wu))
        )
    ]
    for copy in w_copies:
        copy.start()

    barrier = pltpu.get_barrier_semaphore()
    greet = [partner, *ups]
    greet += [device(z, y, x + i, c) for i in (1, 2, 3)] + [device(z, y + i, x, c) for i in (1, 2, 3)]
    for dev in greet:
        pl.semaphore_signal(barrier, inc=1, device_id=dev, device_id_type=MESH)
    w_copies[0].wait()
    w_copies[1].wait()
    pl.semaphore_wait(barrier, len(greet))

    for a in range(2):
        ref = xy.at[a, 0, rows(mine)]
        for i in (1, 3, 2):
            send(ref, ref, x_send.at[a, i - 1], x_recv.at[a, i - 1], device(z, y, x + i, c))
        send(ref, ref, f_send.at[a, 0], f_recv.at[a, 0], partner)

    w_copies[2].wait()
    wdt[...] = wd[...].T

    def row_forward(a):
        for i in (1, 3, 2):
            ref = xy.at[a, 0, rows(c * NX + lax.rem(x - i + NX, NX))]
            arrived(ref, x_send.at[a, i - 1], x_recv.at[a, i - 1])
            send(ref, ref, f_send.at[a, i], f_recv.at[a, i], partner)

    def row_done(a):
        for i in range(4):
            ref = xy.at[a, 0, rows((1 - c) * NX + lax.rem(x - i + NX, NX))]
            arrived(ref, f_send.at[a, i], f_recv.at[a, i])

    half = rows(c * NX, NX)
    other = rows((1 - c) * NX, NX)

    def column_send(a, dists):
        for i in dists:
            send(xy.at[a, 0, half], xy.at[a, 4 - i, half], y_send.at[a, i - 1], y_recv.at[a, i - 1], device(z, y + i, x, c))

    def column_forward(a, dists):
        for i in dists:
            ref = xy.at[a, 4 - i, half]
            arrived(ref, y_send.at[a, i - 1], y_recv.at[a, i - 1])
            send(ref, ref, g_send.at[a, i - 1], g_recv.at[a, i - 1], partner)

    def column_done(a, d):
        arrived(xy.at[a, d, other], g_send.at[a, 3 - d], g_recv.at[a, 3 - d])

    def forward_products(d):
        part[d, GATE] = dot(xy[0, d], wg[...])
        part[d, UP] = dot(xy[0, d], wu[...])

    def grad_products(d):
        part[d, HGRAD] = dot(xy[1, d], wdt[...])

    def span(kind, s, side, d):
        if kind == "gu":
            return (0, 2) if s else ((0, 1), (1, 2))[side]
        return (2, 3) if s or (side == 0) == (d in GROUPS[:2]) else None

    def reduce_step(kind, d, s):
        k = 0 if kind == "gu" else 1
        for side in (0, 1):
            now = span(kind, s, side, d)
            if now is None:
                continue
            j = chunk(4 - s if side == 0 else s - 4)
            before = span(kind, s - 1, side, d) if s else None
            if before is not None:
                lo, hi = before
                arrived(rs_recv.at[side, d, s - 1, lo:hi], r_send.at[side, d, s - 1, k], r_recv.at[side, d, s - 1, k])
            for a in range(*now):
                total = part[d, a, rows(j)]
                if before is not None and before[0] <= a < before[1]:
                    total += rs_recv[side, d, s - 1, a].astype(jnp.float32)
                rs_send[side, d, s, a] = total.astype(jnp.bfloat16)
            lo, hi = now
            send(
                rs_send.at[side, d, s, lo:hi], rs_recv.at[side, d, s, lo:hi],
                r_send.at[side, d, s, k], r_recv.at[side, d, s, k], ups[side],
            )

    def finish(d):
        for side in (0, 1):
            arrived(rs_recv.at[side, d, 3, 0:2], r_send.at[side, d, 3, 0], r_recv.at[side, d, 3, 0])
            arrived(rs_recv.at[side, d, 3, 2:3], r_send.at[side, d, 3, 1], r_recv.at[side, d, 3, 1])
        total = [
            part[d, a, rows(z)] + rs_recv[0, d, 3, a].astype(jnp.float32) + rs_recv[1, d, 3, a].astype(jnp.float32)
            for a in range(3)
        ]
        gate, up_val, hidden_grad = total
        sigma = jax.nn.sigmoid(gate)
        act = gate * sigma
        slope = sigma * (1.0 + gate * (1.0 - sigma))
        pre_gate = hidden_grad * up_val * slope
        pre_up = hidden_grad * act
        back[PRE_GATE, d, rows(z)] = pre_gate.astype(jnp.bfloat16)
        back[HIDDEN, d, rows(z)] = (act * up_val).astype(jnp.bfloat16)
        back[PRE_UP, d, rows(z)] = pre_up.astype(jnp.bfloat16)
        for i, values in enumerate((pre_gate, pre_up)):
            top = jnp.abs(values)
            top = jnp.max(top.reshape(2, 8, top.shape[1]), axis=0)
            best = top[:, 0:128]
            for k in range(1, top.shape[1] // 128):
                best = jnp.maximum(best, top[:, k * 128 : (k + 1) * 128])
            if d != GROUPS[0]:
                best = jnp.maximum(best, pk[0, i * 8 : i * 8 + 8])
            pk[0, i * 8 : i * 8 + 8] = best

    def spread_span(d, t, side):
        if t < 3:
            return 0, 3
        return ((0, 2), (2, 3))[side] if d in GROUPS[:2] else ((0, 1), (1, 3))[side]

    def landed(d, t):
        for side in (0, 1):
            j = chunk(-t - 1 if side == 0 else t + 1)
            lo, hi = spread_span(d, t, side)
            arrived(back.at[lo:hi, d, rows(j)], a_send.at[side, d, t], a_recv.at[side, d, t])

    def spread(d, t):
        if t:
            landed(d, t - 1)
        for side in (0, 1):
            j = chunk(-t if side == 0 else t)
            lo, hi = spread_span(d, t, side)
            ref = back.at[lo:hi, d, rows(j)]
            send(ref, ref, a_send.at[side, d, t], a_recv.at[side, d, t], ups[side])

    row_devs = [device(z, y, x + i % 4, c if i < 4 else 1 - c) for i in range(1, 8)]
    col_devs = [device(z, y + i, x, c) for i in range(1, 4)]
    z_devs = [device(z + i, y, x, c) for i in range(1, 8)]
    stages = ((0, row_devs), (7, col_devs), (10, z_devs))

    def peaks_send(stage):
        first, devs = stages[stage]
        for i, dev in enumerate(devs):
            send(pk.at[stage], pk_recv.at[first + i], p_send.at[first + i], p_recv.at[first + i], dev)

    def peaks_wait(stage):
        first, devs = stages[stage]
        best = pk[stage]
        for i in range(len(devs)):
            arrived(pk_recv.at[first + i], p_send.at[first + i], p_recv.at[first + i])
        for i in range(len(devs)):
            best = jnp.maximum(best, pk_recv[first + i])
        pk[stage + 1] = best

    parts = ((0, 1, -1), (2, -2), (3, -3), (4,))
    starts = (0, 3, 5, 7)

    def input_products(q):
        n = len(parts[q])
        peak_g = jnp.max(pk[3, 0:8]) + 1e-6
        peak_u = jnp.max(pk[3, 8:16]) + 1e-6
        for i, which in enumerate((PRE_GATE, PRE_UP)):
            scale = TOP / (peak_g, peak_u)[i]
            for m, k in enumerate(parts[q]):
                j = chunk(k)
                for d in range(4):
                    values = back[which, d, rows(j)].astype(jnp.float32) * scale
                    row = (d * n + m) * ROWS
                    coded[i, row : row + ROWS] = jnp.clip(values, -FP8_MAX, FP8_MAX).astype(jnp.bfloat16)
        size = 4 * n * ROWS
        first = dot(coded[0, 0:size], wgt[...])
        second = dot(coded[1, 0:size], wut[...])
        total = (peak_g / TOP) * first + (peak_u / TOP) * second
        for d in range(4):
            ig_part[d, starts[q] * ROWS : (starts[q] + n) * ROWS] = total[d * n * ROWS : (d + 1) * n * ROWS].astype(jnp.bfloat16)

    def part_rows(q):
        return slice(starts[q] * ROWS, (starts[q] + len(parts[q])) * ROWS)

    def column_sum_send(q):
        at = part_rows(q)
        for d in (1, 3, 2):
            send(ig_part.at[d, at], ig_recv.at[d, at], c_send.at[q, d - 1], c_recv.at[q, d - 1], device(z, y + d, x, c))

    def row_sum_send(q):
        at = part_rows(q)
        total = ig_part[0, at].astype(jnp.float32)
        for d in (1, 3, 2):
            arrived(ig_recv.at[d, at], c_send.at[q, d - 1], c_recv.at[q, d - 1])
            total += ig_recv[d, at].astype(jnp.float32)
        row_sum[at] = total.astype(jnp.bfloat16)
        for m, k in enumerate(parts[q]):
            j = chunk(k)
            ref = row_sum.at[(starts[q] + m) * ROWS : (starts[q] + m + 1) * ROWS]
            copy = remote(ref, row_recv.at[mine], d_send.at[starts[q] + m], d_recv.at[mine], device(z, y, lax.rem(j, NX), j // NX))

            @pl.when(j != mine)
            def _():
                copy.start()

            @pl.when(j == mine)
            def _():
                row_recv[mine] = ref[...]

    def row_sum_done():
        for q in range(4):
            for m, k in enumerate(parts[q]):
                j = chunk(k)
                ref = row_sum.at[(starts[q] + m) * ROWS : (starts[q] + m + 1) * ROWS]
                copy = remote(ref, row_recv.at[mine], d_send.at[starts[q] + m], d_recv.at[mine], partner)

                @pl.when(j != mine)
                def _():
                    copy.wait_send()

    row_forward(0)
    row_done(0)
    column_send(0, (1, 3))
    w_copies[3].wait()
    w_copies[4].wait()
    forward_products(0)
    reduce_step("gu", 0, 0)
    row_forward(1)
    column_send(1, (1, 3))
    column_send(0, (2,))
    column_send(1, (2,))
    row_done(1)
    grad_products(0)
    reduce_step("gu", 0, 1)
    reduce_step("hg", 0, 0)
    column_forward(0, (1, 3))
    column_done(0, 1)
    forward_products(1)
    reduce_step("gu", 1, 0)
    reduce_step("gu", 0, 2)
    reduce_step("hg", 0, 1)
    column_forward(1, (1, 3))
    column_done(1, 1)
    grad_products(1)
    reduce_step("gu", 1, 1)
    reduce_step("hg", 1, 0)
    column_done(0, 3)
    forward_products(3)
    reduce_step("gu", 3, 0)
    reduce_step("gu", 0, 3)
    reduce_step("hg", 0, 2)
    column_forward(0, (2,))
    column_done(1, 3)
    grad_products(3)
    reduce_step("gu", 1, 2)
    reduce_step("hg", 1, 1)
    reduce_step("gu", 3, 1)
    reduce_step("hg", 3, 0)
    column_done(0, 2)
    forward_products(2)
    reduce_step("gu", 2, 0)
    column_forward(1, (2,))
    reduce_step("hg", 0, 3)
    reduce_step("gu", 1, 3)
    column_done(1, 2)
    grad_products(2)
    reduce_step("hg", 1, 2)
    reduce_step("gu", 3, 2)
    reduce_step("hg", 3, 1)
    reduce_step("gu", 2, 1)
    reduce_step("hg", 2, 0)
    outs = [pltpu.make_async_copy(xy.at[0], tok_out, o_sem.at[0]), pltpu.make_async_copy(xy.at[1], grad_out, o_sem.at[1])]
    for copy in outs:
        copy.start()
    wgt[...] = wg[...].T
    reduce_step("hg", 1, 3)
    reduce_step("gu", 3, 3)
    reduce_step("hg", 3, 2)
    reduce_step("gu", 2, 2)
    reduce_step("hg", 2, 1)
    finish(0)
    spread(0, 0)
    wut[...] = wu[...].T
    reduce_step("hg", 3, 3)
    reduce_step("gu", 2, 3)
    reduce_step("hg", 2, 2)
    finish(1)
    spread(1, 0)
    reduce_step("hg", 2, 3)
    finish(3)
    spread(3, 0)
    spread(0, 1)
    finish(2)
    peaks_send(0)
    spread(2, 0)
    spread(1, 1)
    peaks_wait(0)
    peaks_send(1)
    spread(3, 1)
    peaks_wait(1)
    peaks_send(2)
    spread(2, 1)
    spread(0, 2)
    spread(1, 2)
    peaks_wait(2)
    input_products(0)
    column_sum_send(0)
    spread(3, 2)
    spread(2, 2)
    row_sum_send(0)
    input_products(1)
    column_sum_send(1)
    for d in GROUPS:
        spread(d, 3)
    input_products(2)
    column_sum_send(2)
    row_sum_send(1)
    for d in GROUPS:
        landed(d, 3)
    input_products(3)
    column_sum_send(3)
    copy = pltpu.make_async_copy(back, back_out, o_sem.at[2])
    copy.start()
    outs.append(copy)
    row_sum_send(2)
    row_sum_send(3)
    peak_ref[0] = jnp.max(pk[3, 0:8])
    peak_ref[1] = jnp.max(pk[3, 8:16])
    for i in range(1, 8):
        src = lax.rem(mine + i, 8)
        arrived(row_recv.at[src], d_send.at[0], d_recv.at[src])
    total = row_recv[0].astype(jnp.float32)
    for i in range(1, 8):
        total += row_recv[i].astype(jnp.float32)
    ig_ref[...] = total.astype(jnp.bfloat16)
    row_sum_done()
    for copy in outs:
        copy.wait()
    for copy in sends:
        copy.wait_send()


def weight_kernel(peak_ref, tok_ref, grad_ref, back_ref, gate_ref, up_ref, down_ref, coded):
    tokens = tok_ref.shape[0]
    peak_g, peak_u = peak_ref[0] + 1e-6, peak_ref[1] + 1e-6

    @pl.when(pl.program_id(0) == 0)
    def _():
        for i, (which, peak) in enumerate(((PRE_GATE, peak_g), (PRE_UP, peak_u))):
            values = back_ref[which].astype(jnp.float32) * (TOP / peak)
            coded[i] = jnp.clip(values, -FP8_MAX, FP8_MAX).astype(jnp.bfloat16)

    rows = (((0,), (0,)), ((), ()))
    tok = tok_ref[...]
    for i, (ref, peak) in enumerate(((gate_ref, peak_g), (up_ref, peak_u))):
        ref[...] = ((peak / TOP) * lax.dot_general(tok, coded[i], rows, preferred_element_type=jnp.float32)).astype(jnp.bfloat16)
    down_ref[...] = lax.dot_general(back_ref[HIDDEN], grad_ref[...], rows, preferred_element_type=jnp.float32).astype(jnp.bfloat16)


def local(tokens, gate_weight, up_weight, down_weight, out_grad):
    bf16, f32 = jnp.bfloat16, jnp.float32
    width, hid = gate_weight.shape
    total = NY * 2 * NX * ROWS
    anywhere = pl.BlockSpec(memory_space=pl.ANY)
    vmem, dma = pltpu.VMEM, pltpu.SemaphoreType.DMA
    group = 2 * NX * ROWS
    input_grad, peaks, tok_all, grad_all, back = pl.pallas_call(
        main_kernel,
        name="slab",
        out_shape=(
            jax.ShapeDtypeStruct((ROWS, width), bf16),
            jax.ShapeDtypeStruct((2,), f32),
            jax.ShapeDtypeStruct((NY, group, width), bf16),
            jax.ShapeDtypeStruct((NY, group, width), bf16),
            jax.ShapeDtypeStruct((3, NY, group, hid), bf16),
        ),
        in_specs=[anywhere] * 5,
        out_specs=(
            pl.BlockSpec(memory_space=pltpu.VMEM),
            pl.BlockSpec(memory_space=pltpu.SMEM),
            anywhere,
            anywhere,
            anywhere,
        ),
        scratch_shapes=[
            vmem((2, NY, group, width), bf16),
            vmem((width, hid), bf16),
            vmem((width, hid), bf16),
            vmem((hid, width), bf16),
            vmem((width, hid), bf16),
            vmem((hid, width), bf16),
            vmem((hid, width), bf16),
            vmem((NY, 3, group, hid), f32),
            vmem((2, NY, 4, 3, ROWS, hid), bf16),
            vmem((2, NY, 4, 3, ROWS, hid), bf16),
            vmem((3, NY, group, hid), bf16),
            vmem((2, 3 * NY * ROWS, hid), bf16),
            vmem((NY, NZ * ROWS, width), bf16),
            vmem((NY, NZ * ROWS, width), bf16),
            vmem((NZ * ROWS, width), bf16),
            vmem((8, ROWS, width), bf16),
            vmem((4, 16, 128), f32),
            vmem((17, 16, 128), f32),
            dma((5,)),
            dma((2, 3)), dma((2, 3)), dma((2, 4)), dma((2, 4)), dma((2, 3)), dma((2, 3)), dma((2, 3)), dma((2, 3)),
            dma((2, NY, 4, 2)), dma((2, NY, 4, 2)), dma((2, NY, 4)), dma((2, NY, 4)), dma((17,)), dma((17,)),
            dma((4, 3)), dma((4, 3)), dma((8,)), dma((8,)), dma((3,)),
        ],
        compiler_params=pltpu.CompilerParams(collective_id=0, has_side_effects=True, vmem_limit_bytes=56 * 2**20),
    )(tokens, out_grad, gate_weight, up_weight, down_weight)
    tile = width // 4
    gate_grad, up_grad, down_grad = pl.pallas_call(
        weight_kernel,
        name="weight_grads",
        grid=(4,),
        out_shape=(
            jax.ShapeDtypeStruct((width, hid), bf16),
            jax.ShapeDtypeStruct((width, hid), bf16),
            jax.ShapeDtypeStruct((hid, width), bf16),
        ),
        in_specs=[
            pl.BlockSpec(memory_space=pltpu.SMEM),
            pl.BlockSpec((total, tile), lambda i: (0, i)),
            pl.BlockSpec((total, tile), lambda i: (0, i)),
            pl.BlockSpec((3, total, hid), lambda i: (0, 0, 0)),
        ],
        out_specs=(
            pl.BlockSpec((tile, hid), lambda i: (i, 0)),
            pl.BlockSpec((tile, hid), lambda i: (i, 0)),
            pl.BlockSpec((hid, tile), lambda i: (0, i)),
        ),
        scratch_shapes=[vmem((2, total, hid), bf16)],
        compiler_params=pltpu.CompilerParams(vmem_limit_bytes=48 * 2**20),
    )(peaks, tok_all.reshape(total, width), grad_all.reshape(total, width), back.reshape(3, total, hid))
    return input_grad, gate_grad, up_grad, down_grad, peaks


def solution(mesh):
    in_specs = (P("gy", "gx"), P("gx", "gy"), P("gx", "gy"), P("gy", "gx"), P("gy", "gx"))
    out_specs = (P("gy", "gx"), P("gx", "gy"), P("gx", "gy"), P("gy", "gx"), P())
    return jax.shard_map(local, mesh=mesh, in_specs=in_specs, out_specs=out_specs, check_vma=False)
```

time: 365 us -> 107 us (0.29)
  waiting for transfers between devices: 242 us -> 0 us
  Pallas kernels: 0 us -> 100 us
  blocking collectives: 65.5 us -> 0 us
  matrix products: 28.1 us -> 0 us
  between operations: 15.2 us -> 0.65 us
  other arithmetic: 6.35 us -> 0 us
    pallas_call x0 -> x2, Pallas kernels: none -> 100 us  [the longest x1 93.6 us: local(): pl.pallas_call(main_kernel, name='slab', out_shape=(jax.ShapeDtypeStruct(...]
    all_gather x2 -> x0, waiting for transfers between devices: 97.4 us -> none  [the longest x1 53.9 us: local(): lax.all_gather(tokens, 'gy', axis=0, tiled=True)]
    psum x1 -> x0, waiting for transfers between devices: 84.6 us -> none  [local(): lax.psum(up_part.astype(jnp.bfloat16), 'gx').astype(jnp.float32)]
    pmax x1 -> x0, blocking collectives: 65.5 us -> none  [local(): lax.pmax((jnp.max(jnp.abs(pre_gate)), jnp.max(jnp.abs(pre_up))), 'gy')]
    reduce_scatter x1 -> x0, waiting for transfers between devices: 58.1 us -> none  [local(): lax.psum_scatter((back_gate * first + back_up * second).astype(jnp.bfloat...]
    dot_general x8 -> x0, matrix products: 28.1 us -> none  [the longest x1 4.22 us: local(): lax.dot_general(tok_all, coded_up, rows, preferred_element_type=jnp.float32)]
    reduce_max x1 -> x0, other arithmetic: 4.51 us -> none  [local(): jnp.max(jnp.abs(pre_gate))]
    unnamed x14 -> x12, local copies, waits for them, and re-layouts: 7.72 us -> 6.01 us
  transfers between devices with their start and end apart: 4 -> 0, of which waited for: 4 -> 0; matrix products, arithmetic and copies ran while one was open for 8% -> 0% of each run, Pallas kernels for 0% -> 0%
where the time goes in v1:
time: 107 us
  Pallas kernels  100 us (93%)
  local copies, waits for them, and re-layouts  6.01 us (6%)
    pallas_call x1, Pallas kernels, local(): pl.pallas_call(main_kernel, name='slab', out_shape=(jax.ShapeDtypeStruct(...  93.6 us
    pallas_call x1, Pallas kernels, local(): pl.pallas_call(weight_kernel, name='weight_grads', grid=(4,), out_shape=(...  6.38 us
    unnamed x12, local copies, waits for them, and re-layouts  6.01 us

profile of v1, /device:TPU:1, one launch (start us, length us, event | category | flops | bytes accessed | tf_op | source)
XLA Modules:
  0.0 106.6 jit_solution(10671249447344331730)
XLA Ops:
  0.6 93.6 %slab.1 = (bf16[16,1024]{1,0:T(8,128)(2,1)}, f32[2]{0:T(128)}, bf16[4,128,1024]{2,1,0:T(8,128)(2,1)}, bf16[4,128,1024]{2,1,0:T(8,128)(2,1)}, bf16[3,4,128,896]{3,2,1,0:T(8,128)(2,1)}) custom-call(bf16[16,1024]{1,0:T(8,128)(2,1)} %tok_hbm.1, bf16[16,1024]{1,0:T(8,128)(2,1)} %grad_hbm.1, bf16[1024,896]{1,0:T(8,128)(2,1)} %wg_hbm.1, bf16[1024,896]{1,0:T(8,128)(2,1)} %wu_hbm.1, ...), custom_call_target="tpu_custom_call" | custom-call | tf_op jit(solution)/shard_map/slab/pallas_call | solution.py:423
  94.2 0.0 copy-start
  94.2 1.8 %copy-done = bf16[3,4,128,896]{3,2,1,0:T(8,128)(2,1)S(1)} copy-done((bf16[3,4,128,896]{3,2,1,0:T(8,128)(2,1)S(1)}, bf16[3,4,128,896]{3,2,1,0:T(8,128)(2,1)}, u32[]{:S(2)}) %copy-start) | copy-done | bytes 2752536
  96.0 0.0 copy-start.1
  96.0 1.2 %copy-done.1 = bf16[4,128,1024]{2,1,0:T(8,128)(2,1)S(1)} copy-done((bf16[4,128,1024]{2,1,0:T(8,128)(2,1)S(1)}, bf16[4,128,1024]{2,1,0:T(8,128)(2,1)}, u32[]{:S(2)}) %copy-start.1) | copy-done | bytes 1048600
  97.2 0.0 copy-start.2
  97.2 1.2 %copy-done.2 = bf16[4,128,1024]{2,1,0:T(8,128)(2,1)S(1)} copy-done((bf16[4,128,1024]{2,1,0:T(8,128)(2,1)S(1)}, bf16[4,128,1024]{2,1,0:T(8,128)(2,1)}, u32[]{:S(2)}) %copy-start.2) | copy-done | bytes 1048600
  98.5 0.0 copy-start.3
  98.5 0.7 copy-done.3
  99.1 0.0 copy-start.4
  99.1 6.4 %weight_grads.1 = (bf16[1024,896]{1,0:T(8,128)(2,1)}, bf16[1024,896]{1,0:T(8,128)(2,1)}, bf16[896,1024]{1,0:T(8,128)(2,1)}) custom-call(f32[2]{0:T(128)S(1)} %copy-done.3, bf16[512,1024]{1,0:T(8,128)(2,1)S(1)} %bitcast.4, bf16[512,1024]{1,0:T(8,128)(2,1)S(1)} %bitcast.5, bf16[3,512,896]{2,1,0:T(8,128)(2,1)S(1)} %bitcast.3), custom_call_target="tpu_custom_call" | custom-call | tf_op jit(solution)/shard_map/weight_grads/pallas_call | solution.py:468
  105.5 0.0 copy-done.4
  105.5 0.6 copy.12
  106.1 0.5 copy.13
Async XLA Ops:
  94.2 1.8 %copy-start = (bf16[3,4,128,896]{3,2,1,0:T(8,128)(2,1)S(1)}, bf16[3,4,128,896]{3,2,1,0:T(8,128)(2,1)}, u32[]{:S(2)}) copy-start(bf16[3,4,128,896]{3,2,1,0:T(8,128)(2,1)} %get-tuple-element.17) | copy-start | bytes 8257540
  96.0 1.2 %copy-start.1 = (bf16[4,128,1024]{2,1,0:T(8,128)(2,1)S(1)}, bf16[4,128,1024]{2,1,0:T(8,128)(2,1)}, u32[]{:S(2)}) copy-start(bf16[4,128,1024]{2,1,0:T(8,128)(2,1)} %get-tuple-element.15) | copy-start | bytes 3145732
  97.2 1.2 %copy-start.2 = (bf16[4,128,1024]{2,1,0:T(8,128)(2,1)S(1)}, bf16[4,128,1024]{2,1,0:T(8,128)(2,1)}, u32[]{:S(2)}) copy-start(bf16[4,128,1024]{2,1,0:T(8,128)(2,1)} %get-tuple-element.16) | copy-start | bytes 3145732
  98.5 0.7 copy-start.3
  99.1 6.4 %copy-start.4 = (bf16[16,1024]{1,0:T(8,128)(2,1)S(1)}, bf16[16,1024]{1,0:T(8,128)(2,1)}, u32[]{:S(2)}) copy-start(bf16[16,1024]{1,0:T(8,128)(2,1)} %get-tuple-element.26) | copy-start | bytes 98308

commit v2 on v1

v2 whole, which is shorter than its diff:
```python
import functools

import jax
import jax.numpy as jnp
from jax import lax
from jax.experimental import pallas as pl
from jax.experimental.pallas import tpu as pltpu
from jax.sharding import PartitionSpec as P

MESH = pl.DeviceIdType.MESH
FP8_MAX = 57344.0
HEADROOM = 8.0
TOP = HEADROOM * FP8_MAX
NZ, NY, NX, ROWS = 8, 4, 4, 16
GROUPS = (0, 1, 3, 2)
GATE, UP, HGRAD = 0, 1, 2
PRE_GATE, PRE_UP, HIDDEN = 0, 1, 2


def dot(a, b):
    return jnp.dot(a, b, preferred_element_type=jnp.float32)


def dot_rows(a, b):
    return lax.dot_general(a, b, (((0,), (0,)), ((), ())), preferred_element_type=jnp.float32)


def device(z, y, x, c):
    return (lax.rem(z + NZ, NZ), (lax.rem(y + NY, NY) * NX + lax.rem(x + NX, NX)) * 2 + c)


def main_kernel(
    tok_hbm, grad_hbm, wg_hbm, wu_hbm, wd_hbm,
    ig_ref, peak_ref, gate_out, up_out, hidden_out, grad_out,
    xy, wg, wu, wd, wdt, wgt, wut, part, rs_send, rs_recv, back, coded, w_grad, ig_part, ig_recv, row_sum, row_recv,
    pk, pk_recv,
    w_sem, x_send, x_recv, f_send, f_recv, y_send, y_recv, g_send, g_recv,
    r_send, r_recv, a_send, a_recv, h_send, h_recv, p_send, p_recv, c_send, c_recv, d_send, d_recv, o_sem,
):
    z, gy = lax.axis_index("gx"), lax.axis_index("gy")
    y, x, c = gy // 8, lax.rem(gy // 2, NX), lax.rem(gy, 2)
    mine = c * NX + x
    partner = device(z, y, x, 1 - c)
    ups = (device(z + 1, y, x, c), device(z - 1, y, x, c))
    sends, outs = [], []

    def remote(src, dst, s_sem, r_sem, dev):
        return pltpu.make_async_remote_copy(
            src_ref=src, dst_ref=dst, send_sem=s_sem, recv_sem=r_sem, device_id=dev, device_id_type=MESH
        )

    def send(src, dst, s_sem, r_sem, dev):
        copy = remote(src, dst, s_sem, r_sem, dev)
        copy.start()
        sends.append(copy)

    def arrived(ref, s_sem, r_sem):
        remote(ref, ref, s_sem, r_sem, partner).wait_recv()

    def rows(j, n=1):
        return pl.ds(pl.multiple_of(j * ROWS, ROWS), n * ROWS)

    def of(d, n=1):
        return slice(d * ROWS, (d + n) * ROWS)

    def chunk(k):
        return lax.rem(z + k + 2 * NZ, NZ)

    w_copies = [
        pltpu.make_async_copy(src, dst, w_sem.at[i])
        for i, (src, dst) in enumerate(
            ((tok_hbm, xy.at[0, mine, of(0)]), (grad_hbm, xy.at[1, mine, of(0)]), (wd_hbm, wd), (wg_hbm, wg), (wu_hbm, wu))
        )
    ]
    for copy in w_copies:
        copy.start()

    barrier = pltpu.get_barrier_semaphore()
    greet = [partner, *ups]
    greet += [device(z, y, x + i, c) for i in (1, 2, 3)] + [device(z, y + i, x, c) for i in (1, 2, 3)]
    for dev in greet:
        pl.semaphore_signal(barrier, inc=1, device_id=dev, device_id_type=MESH)
    w_copies[0].wait()
    w_copies[1].wait()
    pl.semaphore_wait(barrier, len(greet))

    def row_send(a):
        ref = xy.at[a, mine, of(0)]
        for i in (1, 3, 2):
            send(ref, ref, x_send.at[a, i - 1], x_recv.at[a, i - 1], device(z, y, x + i, c))
        send(ref, ref, f_send.at[a, 0], f_recv.at[a, 0], partner)

    def column_send(a, piece, dists):
        j = c * NX + lax.rem(x - piece + NX, NX)
        for i in dists:
            send(
                xy.at[a, j, of(0)], xy.at[a, j, of(4 - i)], y_send.at[a, i - 1, piece], y_recv.at[a, i - 1, piece],
                device(z, y + i, x, c),
            )

    def row_forward(a):
        for i in (1, 3, 2):
            ref = xy.at[a, c * NX + lax.rem(x - i + NX, NX), of(0)]
            arrived(ref, x_send.at[a, i - 1], x_recv.at[a, i - 1])
            send(ref, ref, f_send.at[a, i], f_recv.at[a, i], partner)
            column_send(a, i, (1, 3))

    def row_done(a):
        for i in range(4):
            ref = xy.at[a, (1 - c) * NX + lax.rem(x - i + NX, NX), of(0)]
            arrived(ref, f_send.at[a, i], f_recv.at[a, i])

    def half(a, d, core):
        return xy.at[a, pl.ds(core * NX, NX), of(d)]

    def column_forward(a, dists):
        for i in dists:
            for piece in (0, 1, 3, 2):
                ref = xy.at[a, c * NX + lax.rem(x - piece + NX, NX), of(4 - i)]
                arrived(ref, y_send.at[a, i - 1, piece], y_recv.at[a, i - 1, piece])
            ref = half(a, 4 - i, c)
            send(ref, ref, g_send.at[a, i - 1], g_recv.at[a, i - 1], partner)

    def column_done(a, d):
        arrived(half(a, d, 1 - c), g_send.at[a, 3 - d], g_recv.at[a, 3 - d])

    def group(a, d):
        return xy[a, :, of(d)].reshape(2 * NX * ROWS, xy.shape[3])

    def forward_products(d):
        part[d, GATE] = dot(group(0, d), wg[...])
        part[d, UP] = dot(group(0, d), wu[...])

    def grad_products(d):
        part[d, HGRAD] = dot(group(1, d), wdt[...])

    def span(kind, s, side, d):
        if kind == "gu":
            return (0, 2) if s else ((0, 1), (1, 2))[side]
        return (2, 3) if s or (side == 0) == (d in GROUPS[:2]) else None

    def reduce_step(kind, d, s):
        k = 0 if kind == "gu" else 1
        for side in (0, 1):
            now = span(kind, s, side, d)
            if now is None:
                continue
            j = chunk(4 - s if side == 0 else s - 4)
            before = span(kind, s - 1, side, d) if s else None
            if before is not None:
                lo, hi = before
                arrived(rs_recv.at[side, d, s - 1, lo:hi], r_send.at[side, d, s - 1, k], r_recv.at[side, d, s - 1, k])
            for a in range(*now):
                total = part[d, a, rows(j)]
                if before is not None and before[0] <= a < before[1]:
                    total += rs_recv[side, d, s - 1, a].astype(jnp.float32)
                rs_send[side, d, s, a] = total.astype(jnp.bfloat16)
            lo, hi = now
            send(
                rs_send.at[side, d, s, lo:hi], rs_recv.at[side, d, s, lo:hi],
                r_send.at[side, d, s, k], r_recv.at[side, d, s, k], ups[side],
            )

    def finish(d):
        for side in (0, 1):
            arrived(rs_recv.at[side, d, 3, 0:2], r_send.at[side, d, 3, 0], r_recv.at[side, d, 3, 0])
            arrived(rs_recv.at[side, d, 3, 2:3], r_send.at[side, d, 3, 1], r_recv.at[side, d, 3, 1])
        total = [
            part[d, a, rows(z)] + rs_recv[0, d, 3, a].astype(jnp.float32) + rs_recv[1, d, 3, a].astype(jnp.float32)
            for a in range(3)
        ]
        gate, up_val, hidden_grad = total
        sigma = jax.nn.sigmoid(gate)
        act = gate * sigma
        slope = sigma * (1.0 + gate * (1.0 - sigma))
        pre_gate = hidden_grad * up_val * slope
        pre_up = hidden_grad * act
        back[PRE_GATE, z, of(d)] = pre_gate.astype(jnp.bfloat16)
        back[PRE_UP, z, of(d)] = pre_up.astype(jnp.bfloat16)
        back[HIDDEN, z, of(d)] = (act * up_val).astype(jnp.bfloat16)
        for i, values in enumerate((pre_gate, pre_up)):
            top = jnp.abs(values)
            top = jnp.max(top.reshape(2, 8, top.shape[1]), axis=0)
            best = top[:, 0:128]
            for k in range(1, top.shape[1] // 128):
                best = jnp.maximum(best, top[:, k * 128 : (k + 1) * 128])
            if d != GROUPS[0]:
                best = jnp.maximum(best, pk[0, i * 8 : i * 8 + 8])
            pk[0, i * 8 : i * 8 + 8] = best

    def spread_ref(d, t, side):
        j = chunk(-t if side == 0 else t)
        lo, hi = (0, 2) if t < 3 else (side, side + 1)
        return back.at[lo:hi, j, of(d)]

    def landed(d, t):
        for side in (0, 1):
            j = chunk(-t - 1 if side == 0 else t + 1)
            lo, hi = (0, 2) if t < 3 else (side, side + 1)
            arrived(back.at[lo:hi, j, of(d)], a_send.at[side, d, t], a_recv.at[side, d, t])

    def spread(d, t):
        if t:
            landed(d, t - 1)
        for side in (0, 1):
            ref = spread_ref(d, t, side)
            send(ref, ref, a_send.at[side, d, t], a_recv.at[side, d, t], ups[side])

    def hidden_landed(part_of, t):
        for side in (0, 1):
            if t == 3 and side != part_of:
                continue
            j = chunk(-t - 1 if side == 0 else t + 1)
            arrived(back.at[HIDDEN, j, of(2 * part_of, 2)], h_send.at[side, part_of, t], h_recv.at[side, part_of, t])

    def hidden_spread(part_of, t):
        if t:
            hidden_landed(part_of, t - 1)
        for side in (0, 1):
            if t == 3 and side != part_of:
                continue
            ref = back.at[HIDDEN, chunk(-t if side == 0 else t), of(2 * part_of, 2)]
            send(ref, ref, h_send.at[side, part_of, t], h_recv.at[side, part_of, t], ups[side])

    row_devs = [device(z, y, x + i % 4, c if i < 4 else 1 - c) for i in range(1, 8)]
    col_devs = [device(z, y + i, x, c) for i in range(1, 4)]
    z_devs = [device(z + i, y, x, c) for i in range(1, 8)]
    stages = ((0, row_devs), (7, col_devs), (10, z_devs))

    def peaks_send(stage):
        first, devs = stages[stage]
        for i, dev in enumerate(devs):
            send(pk.at[stage], pk_recv.at[first + i], p_send.at[first + i], p_recv.at[first + i], dev)

    def peaks_wait(stage):
        first, devs = stages[stage]
        best = pk[stage]
        for i in range(len(devs)):
            arrived(pk_recv.at[first + i], p_send.at[first + i], p_recv.at[first + i])
        for i in range(len(devs)):
            best = jnp.maximum(best, pk_recv[first + i])
        pk[stage + 1] = best

    def safe_peaks():
        return jnp.max(pk[3, 0:8]) + 1e-6, jnp.max(pk[3, 8:16]) + 1e-6

    parts = ((0, 1, -1), (2, -2), (3, -3), (4,))
    starts = (0, 3, 5, 7)

    def input_products(q):
        peaks = safe_peaks()
        size = 4 * ROWS
        for i, which in enumerate((PRE_GATE, PRE_UP)):
            scale = TOP / peaks[i]
            for k in parts[q]:
                j = chunk(k)
                values = back[which, j].astype(jnp.float32) * scale
                coded[i, j] = jnp.clip(values, -FP8_MAX, FP8_MAX).astype(jnp.bfloat16)
        first, second = (
            dot(jnp.concatenate([coded[i, chunk(k)] for k in parts[q]], axis=0), w[...]) for i, w in enumerate((wgt, wut))
        )
        total = ((peaks[0] / TOP) * first + (peaks[1] / TOP) * second).astype(jnp.bfloat16)
        for m in range(len(parts[q])):
            for d in range(4):
                ig_part[d, of(starts[q] + m)] = total[m * size + d * ROWS : m * size + (d + 1) * ROWS]

    def column_sum_send(q):
        at = of(starts[q], len(parts[q]))
        for d in (1, 3, 2):
            send(ig_part.at[d, at], ig_recv.at[d, at], c_send.at[q, d - 1], c_recv.at[q, d - 1], device(z, y + d, x, c))

    def row_copy(q, m):
        j = chunk(parts[q][m])
        ref = row_sum.at[of(starts[q] + m)]
        k = starts[q] + m
        return j, ref, remote(ref, row_recv.at[mine], d_send.at[k], d_recv.at[mine], device(z, y, lax.rem(j, NX), j // NX))

    def row_sum_send(q):
        at = of(starts[q], len(parts[q]))
        total = ig_part[0, at].astype(jnp.float32)
        for d in (1, 3, 2):
            arrived(ig_recv.at[d, at], c_send.at[q, d - 1], c_recv.at[q, d - 1])
            total += ig_recv[d, at].astype(jnp.float32)
        row_sum[at] = total.astype(jnp.bfloat16)
        for m in range(len(parts[q])):
            j, ref, copy = row_copy(q, m)

            @pl.when(j != mine)
            def _():
                copy.start()

            @pl.when(j == mine)
            def _():
                row_recv[mine] = ref[...]

    def row_sum_finish():
        for i in range(1, 8):
            src = lax.rem(mine + i, 8)
            arrived(row_recv.at[src], d_send.at[0], d_recv.at[src])
        total = row_recv[0].astype(jnp.float32)
        for i in range(1, 8):
            total += row_recv[i].astype(jnp.float32)
        ig_ref[...] = total.astype(jnp.bfloat16)

    def row_sum_sent():
        for q in range(4):
            for m in range(len(parts[q])):
                j, _, copy = row_copy(q, m)

                @pl.when(j != mine)
                def _():
                    copy.wait_send()

    def weight_products(i):
        scale = safe_peaks()[i] / TOP
        width = xy.shape[3]
        total = 2 * NX * 4 * ROWS
        right = coded[i].reshape(total, coded.shape[3])
        for k in range(0, width, 256):
            left = xy[0, :, :, k : k + 256].reshape(total, 256)
            w_grad[i, k : k + 256] = (scale * dot_rows(left, right)).astype(jnp.bfloat16)
        copy = pltpu.make_async_copy(w_grad.at[i], (gate_out, up_out)[i], o_sem.at[i])
        copy.start()
        outs.append(copy)

    def out(src, dst, sem):
        copy = pltpu.make_async_copy(src, dst, o_sem.at[sem])
        copy.start()
        outs.append(copy)

    row_send(0)
    column_send(0, 0, (1, 3))
    row_send(1)
    w_copies[2].wait()
    wdt[...] = wd[...].T
    row_forward(0)
    row_done(0)
    w_copies[3].wait()
    w_copies[4].wait()
    forward_products(0)
    reduce_step("gu", 0, 0)
    column_send(1, 0, (1, 3))
    row_forward(1)
    for piece in range(4):
        column_send(0, piece, (2,))
    for piece in range(4):
        column_send(1, piece, (2,))
    row_done(1)
    grad_products(0)
    reduce_step("hg", 0, 0)
    column_forward(0, (3, 1))
    reduce_step("gu", 0, 1)
    column_done(0, 1)
    forward_products(1)
    reduce_step("gu", 1, 0)
    reduce_step("hg", 0, 1)
    reduce_step("gu", 0, 2)
    column_forward(1, (3, 1))
    column_done(1, 1)
    grad_products(1)
    reduce_step("hg", 1, 0)
    reduce_step("gu", 1, 1)
    reduce_step("hg", 0, 2)
    column_done(0, 3)
    forward_products(3)
    reduce_step("gu", 3, 0)
    reduce_step("gu", 0, 3)
    column_done(1, 3)
    grad_products(3)
    reduce_step("hg", 3, 0)
    reduce_step("gu", 1, 2)
    reduce_step("hg", 1, 1)
    column_forward(0, (2,))
    reduce_step("gu", 3, 1)
    reduce_step("hg", 0, 3)
    column_done(0, 2)
    forward_products(2)
    reduce_step("gu", 2, 0)
    column_forward(1, (2,))
    reduce_step("gu", 1, 3)
    reduce_step("hg", 1, 2)
    reduce_step("gu", 3, 2)
    reduce_step("hg", 3, 1)
    column_done(1, 2)
    grad_products(2)
    reduce_step("hg", 2, 0)
    reduce_step("gu", 2, 1)
    out(xy.at[1], grad_out, 3)
    reduce_step("hg", 1, 3)
    reduce_step("gu", 3, 3)
    reduce_step("hg", 3, 2)
    reduce_step("gu", 2, 2)
    reduce_step("hg", 2, 1)
    finish(0)
    spread(0, 0)
    reduce_step("hg", 3, 3)
    reduce_step("gu", 2, 3)
    reduce_step("hg", 2, 2)
    finish(1)
    spread(1, 0)
    reduce_step("hg", 2, 3)
    finish(3)
    spread(3, 0)
    spread(0, 1)
    wgt[...] = wg[...].T
    finish(2)
    peaks_send(0)
    spread(2, 0)
    spread(1, 1)
    wut[...] = wu[...].T
    peaks_wait(0)
    peaks_send(1)
    spread(3, 1)
    spread(0, 2)
    peaks_wait(1)
    peaks_send(2)
    spread(2, 1)
    spread(1, 2)
    hidden_spread(0, 0)
    hidden_spread(1, 0)
    spread(3, 2)
    spread(2, 2)
    peaks_wait(2)
    input_products(0)
    column_sum_send(0)
    spread(0, 3)
    spread(1, 3)
    input_products(1)
    column_sum_send(1)
    spread(3, 3)
    spread(2, 3)
    hidden_spread(0, 1)
    hidden_spread(1, 1)
    row_sum_send(0)
    input_products(2)
    column_sum_send(2)
    row_sum_send(1)
    for d in GROUPS:
        landed(d, 3)
    input_products(3)
    column_sum_send(3)
    hidden_spread(0, 2)
    hidden_spread(1, 2)
    row_sum_send(2)
    weight_products(0)
    row_sum_send(3)
    hidden_spread(0, 3)
    hidden_spread(1, 3)
    weight_products(1)
    row_sum_finish()
    peak_ref[0] = jnp.max(pk[3, 0:8])
    peak_ref[1] = jnp.max(pk[3, 8:16])
    hidden_landed(0, 3)
    hidden_landed(1, 3)
    out(back.at[HIDDEN], hidden_out, 2)
    row_sum_sent()
    for copy in outs:
        copy.wait()
    for copy in sends:
        copy.wait_send()


def weight_kernel(gate_in, up_in, hidden, out_grad, ig_in, peak_in, gate_ref, up_ref, down_ref, ig_ref, peak_ref, down, sem):
    copies = [pltpu.make_async_copy(gate_in, gate_ref, sem.at[0]), pltpu.make_async_copy(up_in, up_ref, sem.at[1])]
    for copy in copies:
        copy.start()
    for k in range(0, down.shape[0], 256):
        at = slice(k, min(k + 256, down.shape[0]))
        down[at] = dot_rows(hidden[:, at], out_grad[...]).astype(jnp.bfloat16)
        copy = pltpu.make_async_copy(down.at[at], down_ref.at[at], sem.at[len(copies)])
        copy.start()
        copies.append(copy)
    ig_ref[...] = ig_in[...]
    peak_ref[0] = peak_in[0]
    peak_ref[1] = peak_in[1]
    for copy in copies:
        copy.wait()


def local(tokens, gate_weight, up_weight, down_weight, out_grad):
    bf16, f32 = jnp.bfloat16, jnp.float32
    width, hid = gate_weight.shape
    group, size = 2 * NX * ROWS, NY * ROWS
    total = 2 * NX * size
    anywhere = pl.BlockSpec(memory_space=pl.ANY)
    vmem, dma = pltpu.VMEM, pltpu.SemaphoreType.DMA
    args = [pltpu.with_memory_space_constraint(v, pltpu.HBM) for v in (tokens, out_grad, gate_weight, up_weight, down_weight)]
    input_grad, peaks, gate_grad, up_grad, hidden, grad_all = pl.pallas_call(
        main_kernel,
        name="slab",
        out_shape=(
            jax.ShapeDtypeStruct((ROWS, width), bf16),
            jax.ShapeDtypeStruct((2,), f32),
            jax.ShapeDtypeStruct((width, hid), bf16),
            jax.ShapeDtypeStruct((width, hid), bf16),
            jax.ShapeDtypeStruct((2 * NX, size, hid), bf16),
            jax.ShapeDtypeStruct((2 * NX, size, width), bf16),
        ),
        in_specs=[pl.BlockSpec(memory_space=pltpu.HBM)] * 5,
        out_specs=(
            pl.BlockSpec(memory_space=pltpu.VMEM),
            pl.BlockSpec(memory_space=pltpu.SMEM),
            anywhere,
            anywhere,
            anywhere,
            anywhere,
        ),
        scratch_shapes=[
            vmem((2, 2 * NX, size, width), bf16),
            vmem((width, hid), bf16),
            vmem((width, hid), bf16),
            vmem((hid, width), bf16),
            vmem((width, hid), bf16),
            vmem((hid, width), bf16),
            vmem((hid, width), bf16),
            vmem((NY, 3, group, hid), f32),
            vmem((2, NY, 4, 3, ROWS, hid), bf16),
            vmem((2, NY, 4, 3, ROWS, hid), bf16),
            vmem((3, 2 * NX, size, hid), bf16),
            vmem((2, 2 * NX, size, hid), bf16),
            vmem((2, width, hid), bf16),
            vmem((NY, NZ * ROWS, width), bf16),
            vmem((NY, NZ * ROWS, width), bf16),
            vmem((NZ * ROWS, width), bf16),
            vmem((8, ROWS, width), bf16),
            vmem((4, 16, 128), f32),
            vmem((17, 16, 128), f32),
            dma((5,)),
            dma((2, 3)), dma((2, 3)), dma((2, 4)), dma((2, 4)), dma((2, 3, 4)), dma((2, 3, 4)), dma((2, 3)), dma((2, 3)),
            dma((2, NY, 4, 2)), dma((2, NY, 4, 2)), dma((2, NY, 4)), dma((2, NY, 4)), dma((2, 2, 4)), dma((2, 2, 4)),
            dma((17,)), dma((17,)), dma((4, 3)), dma((4, 3)), dma((8,)), dma((8,)), dma((4,)),
        ],
        compiler_params=pltpu.CompilerParams(collective_id=0, has_side_effects=True, vmem_limit_bytes=40 * 2**20),
    )(*args)
    whole = pl.BlockSpec(memory_space=pltpu.VMEM)
    smem = pl.BlockSpec(memory_space=pltpu.SMEM)
    gate_grad, up_grad, down_grad, input_grad, peaks = pl.pallas_call(
        weight_kernel,
        name="weight_grads",
        out_shape=(
            jax.ShapeDtypeStruct((width, hid), bf16),
            jax.ShapeDtypeStruct((width, hid), bf16),
            jax.ShapeDtypeStruct((hid, width), bf16),
            jax.ShapeDtypeStruct((ROWS, width), bf16),
            jax.ShapeDtypeStruct((2,), f32),
        ),
        in_specs=[anywhere, anywhere, whole, whole, whole, smem],
        out_specs=(anywhere, anywhere, anywhere, whole, smem),
        scratch_shapes=[vmem((hid, width), bf16), dma((8,))],
        compiler_params=pltpu.CompilerParams(vmem_limit_bytes=16 * 2**20),
    )(gate_grad, up_grad, hidden.reshape(total, hid), grad_all.reshape(total, width), input_grad, peaks)
    return input_grad, gate_grad, up_grad, down_grad, peaks


def solution(mesh):
    in_specs = (P("gy", "gx"), P("gx", "gy"), P("gx", "gy"), P("gy", "gx"), P("gy", "gx"))
    out_specs = (P("gy", "gx"), P("gx", "gy"), P("gx", "gy"), P("gy", "gx"), P())
    return jax.shard_map(local, mesh=mesh, in_specs=in_specs, out_specs=out_specs, check_vma=False)
```

time: 107 us -> 93.4 us (0.87)
  Pallas kernels: 100 us -> 92.5 us
  local copies, waits for them, and re-layouts: 6.01 us -> 0 us
    unnamed x12 -> x0, local copies, waits for them, and re-layouts: 6.01 us -> none
    pallas_call x1, Pallas kernels: 93.6 us -> 88.9 us  [local(): pl.pallas_call(main_kernel, name='slab', out_shape=(jax.ShapeDtypeStruct(...]
    pallas_call x1, Pallas kernels: 6.38 us -> 3.63 us  [local(): pl.pallas_call(weight_kernel, name='weight_grads', out_shape=(jax.ShapeDt...]
where the time goes in v2:
time: 93.4 us; the launch traced here: 93.3 us
  Pallas kernels  92.5 us (99%)
    pallas_call x1, Pallas kernels, local(): pl.pallas_call(main_kernel, name='slab', out_shape=(jax.ShapeDtypeStruct(...  88.9 us
    pallas_call x1, Pallas kernels, local(): pl.pallas_call(weight_kernel, name='weight_grads', out_shape=(jax.ShapeDt...  3.63 us

profile of v2, /device:TPU:1, one launch (start us, length us, event | category | flops | bytes accessed | tf_op | source)
XLA Modules:
  0.0 93.3 jit_solution(516566358444810150)
XLA Ops:
  0.6 88.9 %slab.1 = (bf16[16,1024]{1,0:T(8,128)(2,1)S(1)}, f32[2]{0:T(128)S(1)}, bf16[1024,896]{1,0:T(8,128)(2,1)S(1)}, bf16[1024,896]{1,0:T(8,128)(2,1)S(1)}, bf16[8,64,8...) custom-call(bf16[16,1024]{1,0:T(8,128)(2,1)} %tok_hbm.1, bf16[16,1024]{1,0:T(8,128)(2,1)} %grad_hbm.1, ...), custom_call_target="tpu_custom_call" | custom-call | tf_op jit(solution)/shard_map/slab/pallas_call | solution.py:488
  89.5 3.6 %weight_grads.1 = (bf16[1024,896]{1,0:T(8,128)(2,1)}, bf16[1024,896]{1,0:T(8,128)(2,1)}, bf16[896,1024]{1,0:T(8,128)(2,1)}, bf16[16,1024]{1,0:T(8,128)(2,1)}, f32[2]{0:T(128)}) custom-call(bf16[1024,896]{1,0:T(8,128)(2,1)S(1)} %get-tuple-element.16.gate_in, bf16[1024,896]{1,0:T(8,128)(2,1)S(1)} %get-tuple-element.17.up_in, bf16[512,896]{1,0:T(8,128)(2,1)S(1)} %bitcast.3, ...), custom_call_target="tpu_custom_call" | custom-call | tf_op jit(solution)/shard_map/weight_grads/pallas_call | solution.py:537

commit v3 on v2

--- a/solution.py
+++ b/solution.py
@@ -13,6 +13,7 @@
 TOP = HEADROOM * FP8_MAX
 NZ, NY, NX, ROWS = 8, 4, 4, 16
 GROUPS = (0, 1, 3, 2)
+FIRST = 0
 GATE, UP, HGRAD = 0, 1, 2
 PRE_GATE, PRE_UP, HIDDEN = 0, 1, 2
 
@@ -32,10 +33,10 @@
 def main_kernel(
     tok_hbm, grad_hbm, wg_hbm, wu_hbm, wd_hbm,
     ig_ref, peak_ref, gate_out, up_out, hidden_out, grad_out,
-    xy, wg, wu, wd, wdt, wgt, wut, part, rs_send, rs_recv, back, coded, w_grad, ig_part, ig_recv, row_sum, row_recv,
+    xy, wg, wu, wd, wdt, wgt, wut, part, rs_send, rs_recv, back, coded, w_grad, ig_part, ig_core, ig_sum, ig_recv, row_sum, row_recv,
     pk, pk_recv,
     w_sem, x_send, x_recv, f_send, f_recv, y_send, y_recv, g_send, g_recv,
-    r_send, r_recv, a_send, a_recv, h_send, h_recv, p_send, p_recv, c_send, c_recv, d_send, d_recv, o_sem,
+    r_send, r_recv, a_send, a_recv, h_send, h_recv, p_send, p_recv, b_send, b_recv, c_send, c_recv, d_send, d_recv, o_sem,
 ):
     z, gy = lax.axis_index("gx"), lax.axis_index("gy")
     y, x, c = gy // 8, lax.rem(gy // 2, NX), lax.rem(gy, 2)
@@ -98,12 +99,15 @@
                 device(z, y + i, x, c),
             )
 
-    def row_forward(a):
-        for i in (1, 3, 2):
-            ref = xy.at[a, c * NX + lax.rem(x - i + NX, NX), of(0)]
-            arrived(ref, x_send.at[a, i - 1], x_recv.at[a, i - 1])
-            send(ref, ref, f_send.at[a, i], f_recv.at[a, i], partner)
-            column_send(a, i, (1, 3))
+    def row_forward(a, i):
+        ref = xy.at[a, c * NX + lax.rem(x - i + NX, NX), of(0)]
+        arrived(ref, x_send.at[a, i - 1], x_recv.at[a, i - 1])
+        send(ref, ref, f_send.at[a, i], f_recv.at[a, i], partner)
+        column_send(a, i, (1, 3))
+
+    def column_far(a):
+        for piece in range(4):
+            column_send(a, piece, (2,))
 
     def row_done(a):
         for i in range(4):
@@ -113,25 +117,40 @@
     def half(a, d, core):
         return xy.at[a, pl.ds(core * NX, NX), of(d)]
 
-    def column_forward(a, dists):
-        for i in dists:
-            for piece in (0, 1, 3, 2):
-                ref = xy.at[a, c * NX + lax.rem(x - piece + NX, NX), of(4 - i)]
-                arrived(ref, y_send.at[a, i - 1, piece], y_recv.at[a, i - 1, piece])
-            ref = half(a, 4 - i, c)
-            send(ref, ref, g_send.at[a, i - 1], g_recv.at[a, i - 1], partner)
+    def column_forward(a, i):
+        for piece in (0, 1, 3, 2):
+            ref = xy.at[a, c * NX + lax.rem(x - piece + NX, NX), of(4 - i)]
+            arrived(ref, y_send.at[a, i - 1, piece], y_recv.at[a, i - 1, piece])
+        ref = half(a, 4 - i, c)
+        send(ref, ref, g_send.at[a, i - 1], g_recv.at[a, i - 1], partner)
 
     def column_done(a, d):
-        arrived(half(a, d, 1 - c), g_send.at[a, 3 - d], g_recv.at[a, 3 - d])
+        if d:
+            arrived(half(a, d, 1 - c), g_send.at[a, 3 - d], g_recv.at[a, 3 - d])
 
     def group(a, d):
         return xy[a, :, of(d)].reshape(2 * NX * ROWS, xy.shape[3])
 
+    def transpose_down():
+        w_copies[2].wait()
+        wdt[...] = wd[...].T
+
+    def transpose_gate():
+        wgt[...] = wg[...].T
+
+    def transpose_up():
+        wut[...] = wu[...].T
+
     def forward_products(d):
+        if d == 0:
+            w_copies[3].wait()
+            w_copies[4].wait()
+        column_done(0, d)
         part[d, GATE] = dot(group(0, d), wg[...])
         part[d, UP] = dot(group(0, d), wu[...])
 
     def grad_products(d):
+        column_done(1, d)
         part[d, HGRAD] = dot(group(1, d), wdt[...])
 
     def span(kind, s, side, d):
@@ -184,7 +203,7 @@
             best = top[:, 0:128]
             for k in range(1, top.shape[1] // 128):
                 best = jnp.maximum(best, top[:, k * 128 : (k + 1) * 128])
-            if d != GROUPS[0]:
+            if d != FIRST:
                 best = jnp.maximum(best, pk[0, i * 8 : i * 8 + 8])
             pk[0, i * 8 : i * 8 + 8] = best
 
@@ -262,12 +281,43 @@
         total = ((peaks[0] / TOP) * first + (peaks[1] / TOP) * second).astype(jnp.bfloat16)
         for m in range(len(parts[q])):
             for d in range(4):
-                ig_part[d, of(starts[q] + m)] = total[m * size + d * ROWS : m * size + (d + 1) * ROWS]
+                ig_part[d // 2, d % 2, of(starts[q] + m)] = total[m * size + d * ROWS : m * size + (d + 1) * ROWS]
+
+    def core_sum_send(q):
+        at = of(starts[q], len(parts[q]))
+        send(ig_part.at[:, 1 - c, at], ig_core.at[:, at], b_send.at[q], b_recv.at[q], partner)
+
+    def column_copy(q, i):
+        at = of(starts[q], len(parts[q]))
+        dev = device(z, y + 2 * i + c, x, c)
+        return remote(ig_sum.at[i, at], ig_recv.at[i, at], c_send.at[q, i], c_recv.at[q, i], dev)
 
     def column_sum_send(q):
         at = of(starts[q], len(parts[q]))
-        for d in (1, 3, 2):
-            send(ig_part.at[d, at], ig_recv.at[d, at], c_send.at[q, d - 1], c_recv.at[q, d - 1], device(z, y + d, x, c))
+        arrived(ig_core.at[:, at], b_send.at[q], b_recv.at[q])
+        for i in (1, 0):
+            total = ig_part[i, c, at].astype(jnp.float32) + ig_core[i, at].astype(jnp.float32)
+            ig_sum[i, at] = total.astype(jnp.bfloat16)
+            copy = column_copy(q, i)
+            if i:
+                copy.start()
+                continue
+
+            @pl.when(c == 1)
+            def _():
+                copy.start()
+
+            @pl.when(c == 0)
+            def _():
+                ig_recv[0, at] = ig_sum[0, at]
+
+    def column_sum_sent():
+        for q in range(4):
+            column_copy(q, 1).wait_send()
+
+            @pl.when(c == 1)
+            def _():
+                column_copy(q, 0).wait_send()
 
     def row_copy(q, m):
         j = chunk(parts[q][m])
@@ -277,10 +327,13 @@
 
     def row_sum_send(q):
         at = of(starts[q], len(parts[q]))
-        total = ig_part[0, at].astype(jnp.float32)
-        for d in (1, 3, 2):
-            arrived(ig_recv.at[d, at], c_send.at[q, d - 1], c_recv.at[q, d - 1])
-            total += ig_recv[d, at].astype(jnp.float32)
+        arrived(ig_recv.at[1, at], c_send.at[q, 1], c_recv.at[q, 1])
+
+        @pl.when(c == 1)
+        def _():
+            arrived(ig_recv.at[0, at], c_send.at[q, 0], c_recv.at[q, 0])
+
+        total = ig_recv[0, at].astype(jnp.float32) + ig_recv[1, at].astype(jnp.float32)
         row_sum[at] = total.astype(jnp.bfloat16)
         for m in range(len(parts[q])):
             j, ref, copy = row_copy(q, m)
@@ -331,128 +384,128 @@
     row_send(0)
     column_send(0, 0, (1, 3))
     row_send(1)
-    w_copies[2].wait()
-    wdt[...] = wd[...].T
-    row_forward(0)
+    column_send(1, 0, (1, 3))
+    row_forward(0, 3)
+    row_forward(0, 1)
+    transpose_down()
+    row_forward(0, 2)
+    column_far(0)
+    row_forward(1, 1)
+    row_forward(1, 3)
     row_done(0)
-    w_copies[3].wait()
-    w_copies[4].wait()
     forward_products(0)
+    row_forward(1, 2)
     reduce_step("gu", 0, 0)
-    column_send(1, 0, (1, 3))
-    row_forward(1)
-    for piece in range(4):
-        column_send(0, piece, (2,))
-    for piece in range(4):
-        column_send(1, piece, (2,))
+    column_forward(0, 1)
+    column_forward(0, 3)
     row_done(1)
     grad_products(0)
     reduce_step("hg", 0, 0)
-    column_forward(0, (3, 1))
-    reduce_step("gu", 0, 1)
-    column_done(0, 1)
-    forward_products(1)
-    reduce_step("gu", 1, 0)
-    reduce_step("hg", 0, 1)
-    reduce_step("gu", 0, 2)
-    column_forward(1, (3, 1))
-    column_done(1, 1)
-    grad_products(1)
-    reduce_step("hg", 1, 0)
-    reduce_step("gu", 1, 1)
-    reduce_step("hg", 0, 2)
-    column_done(0, 3)
     forward_products(3)
     reduce_step("gu", 3, 0)
+    reduce_step("gu", 0, 1)
+    forward_products(1)
+    reduce_step("hg", 0, 1)
+    reduce_step("gu", 1, 0)
+    column_forward(1, 1)
+    column_forward(1, 3)
+    reduce_step("gu", 3, 1)
+    column_forward(0, 2)
+    column_far(1)
+    reduce_step("gu", 0, 2)
+    grad_products(3)
+    reduce_step("hg", 0, 2)
+    reduce_step("hg", 3, 0)
+    reduce_step("gu", 1, 1)
+    grad_products(1)
+    reduce_step("gu", 3, 2)
     reduce_step("gu", 0, 3)
-    column_done(1, 3)
-    grad_products(3)
-    reduce_step("hg", 3, 0)
-    reduce_step("gu", 1, 2)
-    reduce_step("hg", 1, 1)
-    column_forward(0, (2,))
-    reduce_step("gu", 3, 1)
-    reduce_step("hg", 0, 3)
-    column_done(0, 2)
     forward_products(2)
     reduce_step("gu", 2, 0)
-    column_forward(1, (2,))
+    reduce_step("hg", 1, 0)
+    reduce_step("hg", 3, 1)
+    column_forward(1, 2)
+    reduce_step("gu", 1, 2)
+    grad_products(2)
+    out(xy.at[1], grad_out, 3)
+    reduce_step("hg", 2, 0)
+    reduce_step("hg", 0, 3)
+    reduce_step("hg", 1, 1)
+    reduce_step("gu", 2, 1)
+    reduce_step("hg", 3, 2)
+    reduce_step("hg", 2, 1)
+    reduce_step("gu", 3, 3)
+    reduce_step("hg", 1, 2)
+    reduce_step("gu", 2, 2)
+    reduce_step("hg", 2, 2)
+    finish(0)
     reduce_step("gu", 1, 3)
-    reduce_step("hg", 1, 2)
-    reduce_step("gu", 3, 2)
-    reduce_step("hg", 3, 1)
-    column_done(1, 2)
-    grad_products(2)
-    reduce_step("hg", 2, 0)
-    reduce_step("gu", 2, 1)
-    out(xy.at[1], grad_out, 3)
+    reduce_step("hg", 3, 3)
     reduce_step("hg", 1, 3)
-    reduce_step("gu", 3, 3)
-    reduce_step("hg", 3, 2)
-    reduce_step("gu", 2, 2)
-    reduce_step("hg", 2, 1)
-    finish(0)
+    reduce_step("gu", 2, 3)
+    reduce_step("hg", 2, 3)
+    finish(3)
     spread(0, 0)
-    reduce_step("hg", 3, 3)
-    reduce_step("gu", 2, 3)
-    reduce_step("hg", 2, 2)
     finish(1)
     spread(1, 0)
-    reduce_step("hg", 2, 3)
-    finish(3)
     spread(3, 0)
-    spread(0, 1)
-    wgt[...] = wg[...].T
     finish(2)
     peaks_send(0)
     spread(2, 0)
+    hidden_spread(1, 0)
+    spread(3, 1)
     spread(1, 1)
-    wut[...] = wu[...].T
     peaks_wait(0)
     peaks_send(1)
-    spread(3, 1)
-    spread(0, 2)
+    spread(0, 1)
+    spread(2, 1)
     peaks_wait(1)
     peaks_send(2)
-    spread(2, 1)
     spread(1, 2)
+    spread(3, 2)
+    spread(0, 2)
+    spread(2, 2)
+    spread(1, 3)
     hidden_spread(0, 0)
-    hidden_spread(1, 0)
-    spread(3, 2)
-    spread(2, 2)
+    transpose_gate()
+    transpose_up()
+    spread(3, 3)
+    hidden_spread(1, 1)
     peaks_wait(2)
     input_products(0)
+    core_sum_send(0)
+    spread(0, 3)
+    input_products(1)
+    spread(2, 3)
     column_sum_send(0)
-    spread(0, 3)
-    spread(1, 3)
-    input_products(1)
+    hidden_spread(0, 1)
+    core_sum_send(1)
+    input_products(2)
     column_sum_send(1)
-    spread(3, 3)
-    spread(2, 3)
-    hidden_spread(0, 1)
-    hidden_spread(1, 1)
-    row_sum_send(0)
-    input_products(2)
-    column_sum_send(2)
-    row_sum_send(1)
+    core_sum_send(2)
+    hidden_spread(1, 2)
     for d in GROUPS:
         landed(d, 3)
     input_products(3)
+    core_sum_send(3)
+    column_sum_send(2)
+    hidden_spread(0, 2)
     column_sum_send(3)
-    hidden_spread(0, 2)
-    hidden_spread(1, 2)
+    row_sum_send(0)
+    hidden_spread(1, 3)
+    row_sum_send(1)
+    hidden_spread(0, 3)
     row_sum_send(2)
+    row_sum_send(3)
+    weight_products(1)
     weight_products(0)
-    row_sum_send(3)
-    hidden_spread(0, 3)
-    hidden_spread(1, 3)
-    weight_products(1)
+    hidden_landed(0, 3)
+    hidden_landed(1, 3)
+    out(back.at[HIDDEN], hidden_out, 2)
     row_sum_finish()
     peak_ref[0] = jnp.max(pk[3, 0:8])
     peak_ref[1] = jnp.max(pk[3, 8:16])
-    hidden_landed(0, 3)
-    hidden_landed(1, 3)
-    out(back.at[HIDDEN], hidden_out, 2)
+    column_sum_sent()
     row_sum_sent()
     for copy in outs:
         copy.wait()
@@ -461,15 +514,19 @@
 
 
 def weight_kernel(gate_in, up_in, hidden, out_grad, ig_in, peak_in, gate_ref, up_ref, down_ref, ig_ref, peak_ref, down, sem):
-    copies = [pltpu.make_async_copy(gate_in, gate_ref, sem.at[0]), pltpu.make_async_copy(up_in, up_ref, sem.at[1])]
-    for copy in copies:
-        copy.start()
-    for k in range(0, down.shape[0], 256):
-        at = slice(k, min(k + 256, down.shape[0]))
-        down[at] = dot_rows(hidden[:, at], out_grad[...]).astype(jnp.bfloat16)
-        copy = pltpu.make_async_copy(down.at[at], down_ref.at[at], sem.at[len(copies)])
+    copies = []
+
+    def store(src, dst):
+        copy = pltpu.make_async_copy(src, dst, sem.at[len(copies)])
         copy.start()
         copies.append(copy)
+
+    for k in range(0, gate_in.shape[0], 256):
+        store(gate_in.at[k : k + 256], gate_ref.at[k : k + 256])
+        store(up_in.at[k : k + 256], up_ref.at[k : k + 256])
+    for k in range(0, down.shape[0], 128):
+        down[k : k + 128] = dot_rows(hidden[:, k : k + 128], out_grad[...]).astype(jnp.bfloat16)
+        store(down.at[k : k + 128], down_ref.at[k : k + 128])
     ig_ref[...] = ig_in[...]
     peak_ref[0] = peak_in[0]
     peak_ref[1] = peak_in[1]
@@ -519,8 +576,10 @@
             vmem((3, 2 * NX, size, hid), bf16),
             vmem((2, 2 * NX, size, hid), bf16),
             vmem((2, width, hid), bf16),
-            vmem((NY, NZ * ROWS, width), bf16),
-            vmem((NY, NZ * ROWS, width), bf16),
+            vmem((2, 2, NZ * ROWS, width), bf16),
+            vmem((2, NZ * ROWS, width), bf16),
+            vmem((2, NZ * ROWS, width), bf16),
+            vmem((2, NZ * ROWS, width), bf16),
             vmem((NZ * ROWS, width), bf16),
             vmem((8, ROWS, width), bf16),
             vmem((4, 16, 128), f32),
@@ -528,7 +587,7 @@
             dma((5,)),
             dma((2, 3)), dma((2, 3)), dma((2, 4)), dma((2, 4)), dma((2, 3, 4)), dma((2, 3, 4)), dma((2, 3)), dma((2, 3)),
             dma((2, NY, 4, 2)), dma((2, NY, 4, 2)), dma((2, NY, 4)), dma((2, NY, 4)), dma((2, 2, 4)), dma((2, 2, 4)),
-            dma((17,)), dma((17,)), dma((4, 3)), dma((4, 3)), dma((8,)), dma((8,)), dma((4,)),
+            dma((17,)), dma((17,)), dma((4,)), dma((4,)), dma((4, 2)), dma((4, 2)), dma((8,)), dma((8,)), dma((5,)),
         ],
         compiler_params=pltpu.CompilerParams(collective_id=0, has_side_effects=True, vmem_limit_bytes=40 * 2**20),
     )(*args)
@@ -546,7 +605,7 @@
         ),
         in_specs=[anywhere, anywhere, whole, whole, whole, smem],
         out_specs=(anywhere, anywhere, anywhere, whole, smem),
-        scratch_shapes=[vmem((hid, width), bf16), dma((8,))],
+        scratch_shapes=[vmem((hid, width), bf16), dma((16,))],
         compiler_params=pltpu.CompilerParams(vmem_limit_bytes=16 * 2**20),
     )(gate_grad, up_grad, hidden.reshape(total, hid), grad_all.reshape(total, width), input_grad, peaks)
     return input_grad, gate_grad, up_grad, down_grad, peaks

time: 93.4 us -> 90.2 us (0.966)
  Pallas kernels: 92.5 us -> 89.3 us
    pallas_call x1, Pallas kernels: 88.9 us -> 85.6 us  [local(): pl.pallas_call(main_kernel, name='slab', out_shape=(jax.ShapeDtypeStruct(...]
where the time goes in v3:
time: 90.2 us; the launch traced here: 90.1 us
  Pallas kernels  89.3 us (99%)
    pallas_call x1, Pallas kernels, local(): pl.pallas_call(main_kernel, name='slab', out_shape=(jax.ShapeDtypeStruct(...  85.6 us
    pallas_call x1, Pallas kernels, local(): pl.pallas_call(weight_kernel, name='weight_grads', out_shape=(jax.ShapeDt...  3.7 us

profile of v3, /device:TPU:1, one launch (start us, length us, event | category | flops | bytes accessed | tf_op | source)
XLA Modules:
  0.0 90.1 jit_solution(4720643546754739224)
XLA Ops:
  0.6 85.6 %slab.1 = (bf16[16,1024]{1,0:T(8,128)(2,1)S(1)}, f32[2]{0:T(128)S(1)}, bf16[1024,896]{1,0:T(8,128)(2,1)S(1)}, bf16[1024,896]{1,0:T(8,128)(2,1)S(1)}, bf16[8,64,8...) custom-call(bf16[16,1024]{1,0:T(8,128)(2,1)} %tok_hbm.1, bf16[16,1024]{1,0:T(8,128)(2,1)} %grad_hbm.1, ...), custom_call_target="tpu_custom_call" | custom-call | tf_op jit(solution)/shard_map/slab/pallas_call | solution.py:545
  86.2 3.7 %weight_grads.1 = (bf16[1024,896]{1,0:T(8,128)(2,1)}, bf16[1024,896]{1,0:T(8,128)(2,1)}, bf16[896,1024]{1,0:T(8,128)(2,1)}, bf16[16,1024]{1,0:T(8,128)(2,1)}, f32[2]{0:T(128)}) custom-call(bf16[1024,896]{1,0:T(8,128)(2,1)S(1)} %get-tuple-element.16.gate_in, bf16[1024,896]{1,0:T(8,128)(2,1)S(1)} %get-tuple-element.17.up_in, bf16[512,896]{1,0:T(8,128)(2,1)S(1)} %bitcast.3, ...), custom_call_target="tpu_custom_call" | custom-call | tf_op jit(solution)/shard_map/weight_grads/pallas_call | solution.py:596

commit v4 on v3

--- a/solution.py
+++ b/solution.py
@@ -203,9 +203,10 @@
             best = top[:, 0:128]
             for k in range(1, top.shape[1] // 128):
                 best = jnp.maximum(best, top[:, k * 128 : (k + 1) * 128])
+            best = jnp.max(best, axis=0, keepdims=True)
             if d != FIRST:
-                best = jnp.maximum(best, pk[0, i * 8 : i * 8 + 8])
-            pk[0, i * 8 : i * 8 + 8] = best
+                best = jnp.maximum(best, pk[0, i : i + 1])
+            pk[0, i : i + 1] = best
 
     def spread_ref(d, t, side):
         j = chunk(-t if side == 0 else t)
@@ -261,7 +262,7 @@
         pk[stage + 1] = best
 
     def safe_peaks():
-        return jnp.max(pk[3, 0:8]) + 1e-6, jnp.max(pk[3, 8:16]) + 1e-6
+        return jnp.max(pk[3, 0:1]) + 1e-6, jnp.max(pk[3, 1:2]) + 1e-6
 
     parts = ((0, 1, -1), (2, -2), (3, -3), (4,))
     starts = (0, 3, 5, 7)
@@ -503,8 +504,8 @@
     hidden_landed(1, 3)
     out(back.at[HIDDEN], hidden_out, 2)
     row_sum_finish()
-    peak_ref[0] = jnp.max(pk[3, 0:8])
-    peak_ref[1] = jnp.max(pk[3, 8:16])
+    peak_ref[0] = jnp.max(pk[3, 0:1])
+    peak_ref[1] = jnp.max(pk[3, 1:2])
     column_sum_sent()
     row_sum_sent()
     for copy in outs:
@@ -582,8 +583,8 @@
             vmem((2, NZ * ROWS, width), bf16),
             vmem((NZ * ROWS, width), bf16),
             vmem((8, ROWS, width), bf16),
-            vmem((4, 16, 128), f32),
-            vmem((17, 16, 128), f32),
+            vmem((4, 2, 128), f32),
+            vmem((17, 2, 128), f32),
             dma((5,)),
             dma((2, 3)), dma((2, 3)), dma((2, 4)), dma((2, 4)), dma((2, 3, 4)), dma((2, 3, 4)), dma((2, 3)), dma((2, 3)),
             dma((2, NY, 4, 2)), dma((2, NY, 4, 2)), dma((2, NY, 4)), dma((2, NY, 4)), dma((2, 2, 4)), dma((2, 2, 4)),

time: 90.2 us -> 89 us (0.987)
  Pallas kernels: 89.3 us -> 88.2 us
    pallas_call x1, Pallas kernels: 85.6 us -> 84.5 us  [local(): pl.pallas_call(main_kernel, name='slab', out_shape=(jax.ShapeDtypeStruct(...]
where the time goes in v4:
time: 89 us
  Pallas kernels  88.2 us (99%)
    pallas_call x1, Pallas kernels, local(): pl.pallas_call(main_kernel, name='slab', out_shape=(jax.ShapeDtypeStruct(...  84.5 us
    pallas_call x1, Pallas kernels, local(): pl.pallas_call(weight_kernel, name='weight_grads', out_shape=(jax.ShapeDt...  3.7 us

profile of v4, /device:TPU:1, one launch (start us, length us, event | category | flops | bytes accessed | tf_op | source)
XLA Modules:
  0.0 89.0 jit_solution(179748038209223315)
XLA Ops:
  0.6 84.5 %slab.1 = (bf16[16,1024]{1,0:T(8,128)(2,1)S(1)}, f32[2]{0:T(128)S(1)}, bf16[1024,896]{1,0:T(8,128)(2,1)S(1)}, bf16[1024,896]{1,0:T(8,128)(2,1)S(1)}, bf16[8,64,8...) custom-call(bf16[16,1024]{1,0:T(8,128)(2,1)} %tok_hbm.1, bf16[16,1024]{1,0:T(8,128)(2,1)} %grad_hbm.1, ...), custom_call_target="tpu_custom_call" | custom-call | tf_op jit(solution)/shard_map/slab/pallas_call | solution.py:546
  85.1 3.7 %weight_grads.1 = (bf16[1024,896]{1,0:T(8,128)(2,1)}, bf16[1024,896]{1,0:T(8,128)(2,1)}, bf16[896,1024]{1,0:T(8,128)(2,1)}, bf16[16,1024]{1,0:T(8,128)(2,1)}, f32[2]{0:T(128)}) custom-call(bf16[1024,896]{1,0:T(8,128)(2,1)S(1)} %get-tuple-element.16.gate_in, bf16[1024,896]{1,0:T(8,128)(2,1)S(1)} %get-tuple-element.17.up_in, bf16[512,896]{1,0:T(8,128)(2,1)S(1)} %bitcast.3, ...), custom_call_target="tpu_custom_call" | custom-call | tf_op jit(solution)/shard_map/weight_grads/pallas_call | solution.py:597

commit v5 on v4

--- a/solution.py
+++ b/solution.py
@@ -33,10 +33,10 @@
 def main_kernel(
     tok_hbm, grad_hbm, wg_hbm, wu_hbm, wd_hbm,
     ig_ref, peak_ref, gate_out, up_out, hidden_out, grad_out,
-    xy, wg, wu, wd, wdt, wgt, wut, part, rs_send, rs_recv, back, coded, w_grad, ig_part, ig_core, ig_sum, ig_recv, row_sum, row_recv,
+    xy, wg, wu, wd, wdt, wgt, wut, part, rs_send, rs_recv, back, coded, w_grad, ig_part, ig_core, ig_sum, ig_recv, ig_last, row_sum, row_recv,
     pk, pk_recv,
     w_sem, x_send, x_recv, f_send, f_recv, y_send, y_recv, g_send, g_recv,
-    r_send, r_recv, a_send, a_recv, h_send, h_recv, p_send, p_recv, b_send, b_recv, c_send, c_recv, d_send, d_recv, o_sem,
+    r_send, r_recv, a_send, a_recv, h_send, h_recv, p_send, p_recv, b_send, b_recv, c_send, c_recv, l_send, l_recv, d_send, d_recv, o_sem,
 ):
     z, gy = lax.axis_index("gx"), lax.axis_index("gy")
     y, x, c = gy // 8, lax.rem(gy // 2, NX), lax.rem(gy, 2)
@@ -284,6 +284,11 @@
             for d in range(4):
                 ig_part[d // 2, d % 2, of(starts[q] + m)] = total[m * size + d * ROWS : m * size + (d + 1) * ROWS]
 
+    def last_sum_send():
+        at = of(starts[3], len(parts[3]))
+        for d in (2, 1, 3):
+            send(ig_part.at[d // 2, d % 2, at], ig_last.at[d - 1], l_send.at[d - 1], l_recv.at[d - 1], device(z, y + d, x, c))
+
     def core_sum_send(q):
         at = of(starts[q], len(parts[q]))
         send(ig_part.at[:, 1 - c, at], ig_core.at[:, at], b_send.at[q], b_recv.at[q], partner)
@@ -313,7 +318,7 @@
                 ig_recv[0, at] = ig_sum[0, at]
 
     def column_sum_sent():
-        for q in range(4):
+        for q in range(3):
             column_copy(q, 1).wait_send()
 
             @pl.when(c == 1)
@@ -328,13 +333,19 @@
 
     def row_sum_send(q):
         at = of(starts[q], len(parts[q]))
-        arrived(ig_recv.at[1, at], c_send.at[q, 1], c_recv.at[q, 1])
-
-        @pl.when(c == 1)
-        def _():
-            arrived(ig_recv.at[0, at], c_send.at[q, 0], c_recv.at[q, 0])
-
-        total = ig_recv[0, at].astype(jnp.float32) + ig_recv[1, at].astype(jnp.float32)
+        if q == 3:
+            total = ig_part[0, 0, at].astype(jnp.float32)
+            for d in (1, 3, 2):
+                arrived(ig_last.at[d - 1], l_send.at[d - 1], l_recv.at[d - 1])
+                total += ig_last[d - 1].astype(jnp.float32)
+        else:
+            arrived(ig_recv.at[1, at], c_send.at[q, 1], c_recv.at[q, 1])
+
+            @pl.when(c == 1)
+            def _():
+                arrived(ig_recv.at[0, at], c_send.at[q, 0], c_recv.at[q, 0])
+
+            total = ig_recv[0, at].astype(jnp.float32) + ig_recv[1, at].astype(jnp.float32)
         row_sum[at] = total.astype(jnp.bfloat16)
         for m in range(len(parts[q])):
             j, ref, copy = row_copy(q, m)
@@ -383,12 +394,12 @@
         outs.append(copy)
 
     row_send(0)
+    transpose_down()
+    row_send(1)
     column_send(0, 0, (1, 3))
-    row_send(1)
     column_send(1, 0, (1, 3))
     row_forward(0, 3)
     row_forward(0, 1)
-    transpose_down()
     row_forward(0, 2)
     column_far(0)
     row_forward(1, 1)
@@ -397,106 +408,105 @@
     forward_products(0)
     row_forward(1, 2)
     reduce_step("gu", 0, 0)
+    column_forward(0, 3)
+    column_far(1)
     column_forward(0, 1)
-    column_forward(0, 3)
     row_done(1)
     grad_products(0)
     reduce_step("hg", 0, 0)
+    forward_products(1)
+    reduce_step("gu", 1, 0)
+    reduce_step("gu", 0, 1)
     forward_products(3)
+    reduce_step("hg", 0, 1)
+    column_forward(1, 1)
     reduce_step("gu", 3, 0)
-    reduce_step("gu", 0, 1)
-    forward_products(1)
-    reduce_step("hg", 0, 1)
-    reduce_step("gu", 1, 0)
-    column_forward(1, 1)
+    reduce_step("gu", 1, 1)
     column_forward(1, 3)
+    column_forward(0, 2)
+    grad_products(3)
+    reduce_step("hg", 3, 0)
+    reduce_step("gu", 0, 2)
+    grad_products(1)
+    reduce_step("hg", 0, 2)
+    column_forward(1, 2)
     reduce_step("gu", 3, 1)
-    column_forward(0, 2)
-    column_far(1)
-    reduce_step("gu", 0, 2)
-    grad_products(3)
-    reduce_step("hg", 0, 2)
-    reduce_step("hg", 3, 0)
-    reduce_step("gu", 1, 1)
-    grad_products(1)
-    reduce_step("gu", 3, 2)
-    reduce_step("gu", 0, 3)
+    reduce_step("hg", 1, 0)
     forward_products(2)
-    reduce_step("gu", 2, 0)
-    reduce_step("hg", 1, 0)
-    reduce_step("hg", 3, 1)
-    column_forward(1, 2)
     reduce_step("gu", 1, 2)
     grad_products(2)
     out(xy.at[1], grad_out, 3)
+    reduce_step("gu", 0, 3)
+    reduce_step("gu", 2, 0)
     reduce_step("hg", 2, 0)
     reduce_step("hg", 0, 3)
     reduce_step("hg", 1, 1)
+    transpose_up()
+    reduce_step("hg", 3, 1)
+    reduce_step("gu", 3, 2)
     reduce_step("gu", 2, 1)
+    reduce_step("hg", 2, 1)
+    finish(0)
+    reduce_step("hg", 1, 2)
+    reduce_step("gu", 1, 3)
     reduce_step("hg", 3, 2)
-    reduce_step("hg", 2, 1)
-    reduce_step("gu", 3, 3)
-    reduce_step("hg", 1, 2)
     reduce_step("gu", 2, 2)
     reduce_step("hg", 2, 2)
-    finish(0)
-    reduce_step("gu", 1, 3)
+    reduce_step("hg", 1, 3)
+    reduce_step("gu", 3, 3)
     reduce_step("hg", 3, 3)
-    reduce_step("hg", 1, 3)
     reduce_step("gu", 2, 3)
     reduce_step("hg", 2, 3)
-    finish(3)
     spread(0, 0)
     finish(1)
+    finish(3)
+    spread(3, 0)
     spread(1, 0)
-    spread(3, 0)
     finish(2)
     peaks_send(0)
     spread(2, 0)
-    hidden_spread(1, 0)
+    spread(0, 1)
+    hidden_spread(0, 0)
+    spread(1, 1)
+    transpose_gate()
     spread(3, 1)
-    spread(1, 1)
     peaks_wait(0)
     peaks_send(1)
-    spread(0, 1)
     spread(2, 1)
     peaks_wait(1)
     peaks_send(2)
+    spread(0, 2)
+    spread(3, 2)
     spread(1, 2)
-    spread(3, 2)
-    spread(0, 2)
     spread(2, 2)
-    spread(1, 3)
-    hidden_spread(0, 0)
-    transpose_gate()
-    transpose_up()
-    spread(3, 3)
-    hidden_spread(1, 1)
+    hidden_spread(1, 0)
+    hidden_spread(0, 1)
+    spread(0, 3)
     peaks_wait(2)
     input_products(0)
     core_sum_send(0)
-    spread(0, 3)
+    spread(3, 3)
     input_products(1)
+    column_sum_send(0)
+    core_sum_send(1)
+    spread(1, 3)
     spread(2, 3)
-    column_sum_send(0)
-    hidden_spread(0, 1)
-    core_sum_send(1)
+    hidden_spread(1, 1)
     input_products(2)
+    core_sum_send(2)
     column_sum_send(1)
-    core_sum_send(2)
-    hidden_spread(1, 2)
+    hidden_spread(0, 2)
+    column_sum_send(2)
     for d in GROUPS:
         landed(d, 3)
     input_products(3)
-    core_sum_send(3)
-    column_sum_send(2)
-    hidden_spread(0, 2)
-    column_sum_send(3)
+    hidden_spread(1, 2)
+    last_sum_send()
     row_sum_send(0)
-    hidden_spread(1, 3)
     row_sum_send(1)
     hidden_spread(0, 3)
     row_sum_send(2)
+    hidden_spread(1, 3)
     row_sum_send(3)
     weight_products(1)
     weight_products(0)
@@ -581,6 +591,7 @@
             vmem((2, NZ * ROWS, width), bf16),
             vmem((2, NZ * ROWS, width), bf16),
             vmem((2, NZ * ROWS, width), bf16),
+            vmem((3, ROWS, width), bf16),
             vmem((NZ * ROWS, width), bf16),
             vmem((8, ROWS, width), bf16),
             vmem((4, 2, 128), f32),
@@ -588,7 +599,7 @@
             dma((5,)),
             dma((2, 3)), dma((2, 3)), dma((2, 4)), dma((2, 4)), dma((2, 3, 4)), dma((2, 3, 4)), dma((2, 3)), dma((2, 3)),
             dma((2, NY, 4, 2)), dma((2, NY, 4, 2)), dma((2, NY, 4)), dma((2, NY, 4)), dma((2, 2, 4)), dma((2, 2, 4)),
-            dma((17,)), dma((17,)), dma((4,)), dma((4,)), dma((4, 2)), dma((4, 2)), dma((8,)), dma((8,)), dma((5,)),
+            dma((17,)), dma((17,)), dma((3,)), dma((3,)), dma((3, 2)), dma((3, 2)), dma((3,)), dma((3,)), dma((8,)), dma((8,)), dma((5,)),
         ],
         compiler_params=pltpu.CompilerParams(collective_id=0, has_side_effects=True, vmem_limit_bytes=40 * 2**20),
     )(*args)

time: 89 us -> 88.1 us (0.990)
  Pallas kernels: 88.2 us -> 87.2 us
    pallas_call x1, Pallas kernels: 84.5 us -> 83.5 us  [local(): pl.pallas_call(main_kernel, name='slab', out_shape=(jax.ShapeDtypeStruct(...]
where the time goes in v5:
time: 88.1 us; the launch traced here: 88 us
  Pallas kernels  87.2 us (99%)
    pallas_call x1, Pallas kernels, local(): pl.pallas_call(main_kernel, name='slab', out_shape=(jax.ShapeDtypeStruct(...  83.5 us
    pallas_call x1, Pallas kernels, local(): pl.pallas_call(weight_kernel, name='weight_grads', out_shape=(jax.ShapeDt...  3.7 us

profile of v5, /device:TPU:1, one launch (start us, length us, event | category | flops | bytes accessed | tf_op | source)
XLA Modules:
  0.0 88.0 jit_solution(589825950075529106)
XLA Ops:
  0.6 83.5 %slab.1 = (bf16[16,1024]{1,0:T(8,128)(2,1)S(1)}, f32[2]{0:T(128)S(1)}, bf16[1024,896]{1,0:T(8,128)(2,1)S(1)}, bf16[1024,896]{1,0:T(8,128)(2,1)S(1)}, bf16[8,64,8...) custom-call(bf16[16,1024]{1,0:T(8,128)(2,1)} %tok_hbm.1, bf16[16,1024]{1,0:T(8,128)(2,1)} %grad_hbm.1, ...), custom_call_target="tpu_custom_call" | custom-call | tf_op jit(solution)/shard_map/slab/pallas_call | solution.py:556
  84.2 3.7 %weight_grads.1 = (bf16[1024,896]{1,0:T(8,128)(2,1)}, bf16[1024,896]{1,0:T(8,128)(2,1)}, bf16[896,1024]{1,0:T(8,128)(2,1)}, bf16[16,1024]{1,0:T(8,128)(2,1)}, f32[2]{0:T(128)}) custom-call(bf16[1024,896]{1,0:T(8,128)(2,1)S(1)} %get-tuple-element.16.gate_in, bf16[1024,896]{1,0:T(8,128)(2,1)S(1)} %get-tuple-element.17.up_in, bf16[512,896]{1,0:T(8,128)(2,1)S(1)} %bitcast.3, ...), custom_call_target="tpu_custom_call" | custom-call | tf_op jit(solution)/shard_map/weight_grads/pallas_call | solution.py:608

commit v6 on v5

--- a/solution.py
+++ b/solution.py
@@ -392,6 +392,11 @@
         copy = pltpu.make_async_copy(src, dst, o_sem.at[sem])
         copy.start()
         outs.append(copy)
+
+    def settle(keep):
+        for copy in sends[: len(sends) - keep]:
+            copy.wait_send()
+        del sends[: len(sends) - keep]
 
     row_send(0)
     transpose_down()
@@ -482,6 +487,7 @@
     hidden_spread(1, 0)
     hidden_spread(0, 1)
     spread(0, 3)
+    settle(16)
     peaks_wait(2)
     input_products(0)
     core_sum_send(0)
@@ -503,6 +509,7 @@
     hidden_spread(1, 2)
     last_sum_send()
     row_sum_send(0)
+    settle(16)
     row_sum_send(1)
     hidden_spread(0, 3)
     row_sum_send(2)

time: 88.1 us -> 87.9 us (level)
  no operation moved by 1% of the time
where the time goes in v6:
time: 87.9 us; the launch traced here: 87.8 us
  Pallas kernels  87 us (99%)
    pallas_call x1, Pallas kernels, local(): pl.pallas_call(main_kernel, name='slab', out_shape=(jax.ShapeDtypeStruct(...  83.3 us
    pallas_call x1, Pallas kernels, local(): pl.pallas_call(weight_kernel, name='weight_grads', out_shape=(jax.ShapeDt...  3.7 us

profile of v6, /device:TPU:1, one launch (start us, length us, event | category | flops | bytes accessed | tf_op | source)
XLA Modules:
  0.0 87.8 jit_solution(14879335300931906832)
XLA Ops:
  0.6 83.3 %slab.1 = (bf16[16,1024]{1,0:T(8,128)(2,1)S(1)}, f32[2]{0:T(128)S(1)}, bf16[1024,896]{1,0:T(8,128)(2,1)S(1)}, bf16[1024,896]{1,0:T(8,128)(2,1)S(1)}, bf16[8,64,8...) custom-call(bf16[16,1024]{1,0:T(8,128)(2,1)} %tok_hbm.1, bf16[16,1024]{1,0:T(8,128)(2,1)} %grad_hbm.1, ...), custom_call_target="tpu_custom_call" | custom-call | tf_op jit(solution)/shard_map/slab/pallas_call | solution.py:563
  83.9 3.7 %weight_grads.1 = (bf16[1024,896]{1,0:T(8,128)(2,1)}, bf16[1024,896]{1,0:T(8,128)(2,1)}, bf16[896,1024]{1,0:T(8,128)(2,1)}, bf16[16,1024]{1,0:T(8,128)(2,1)}, f32[2]{0:T(128)}) custom-call(bf16[1024,896]{1,0:T(8,128)(2,1)S(1)} %get-tuple-element.16.gate_in, bf16[1024,896]{1,0:T(8,128)(2,1)S(1)} %get-tuple-element.17.up_in, bf16[512,896]{1,0:T(8,128)(2,1)S(1)} %bitcast.3, ...), custom_call_target="tpu_custom_call" | custom-call | tf_op jit(solution)/shard_map/weight_grads/pallas_call | solution.py:615
